TPU v7x, 256 devices: a whole 4x4x8 slice. The times are simulated.
256 devices in a mesh: node: 16 (over y, x_hi, core), cross: 16 (over x_lo, z).
Axes of the slice: x: 4 (x_hi: 2, x_lo: 2; x = x_hi * 2 + x_lo), y: 4, z: 8, core: 2. Of those that a mesh axis runs over, the one named last changes fastest.
Arguments:
- activations: bfloat16 [65536, 8192], P(('node', 'cross')), may hold values from -24 to 24
- queries: bfloat16 [65536, 4096], P(('node', 'cross')), may hold values from -150 to 150
- keys: bfloat16 [65536, 512], P(('node', 'cross')), may hold values from -6 to 6
- segment_ids: int32 [256, 256], P(('node', 'cross')), may hold values from 0 to 3, never falling along the last dimension, each value on 1 to 128 neighbouring positions
- cotangent: bfloat16 [65536, 4096], P(('node', 'cross')), may hold values from -6 to 6
- value_codes: bfloat16 [8192, 512], P(('node', 'cross')), may hold values from -127 to 127
- value_scales: float32 [8192, 4], P(('node', 'cross')), may hold values from 5e-05 to 0.00045
Outputs:
- attended: bfloat16 [65536, 4096], P(('node', 'cross'))
- weight_grad: float32 [8192, 512], P(('node', 'cross'))
All inputs are finite; a program needn't handle non-finite values.
Results may differ from a plain program's by a relative error of at most 0.017.
Values may be sent and summed in bfloat16 or wider, within the bound.
No kernel may reach another device: no remote copies, remote signals or barrier semaphores. Data moves between devices by JAX's collectives and lax.ppermute only.
A program may use at most 128 MiB of HBM per device.

v0:
```python
import math

import jax
import jax.numpy as jnp
from jax import lax
from jax.sharding import PartitionSpec as P


def attention_weights(query_rows, key_rows, segment, kv_heads, head_dim):
    length = query_rows.shape[0]
    group = query_rows.shape[1] // (kv_heads * head_dim)
    query_b = query_rows.reshape(length, kv_heads, group, head_dim)
    key_b = key_rows.reshape(length, kv_heads, head_dim)
    scores = jnp.einsum(
        "tgcd,sgd->gcts", query_b, key_b, preferred_element_type=jnp.float32
    ) / math.sqrt(head_dim)
    position = jnp.arange(length)
    allowed = (position[None, :] <= position[:, None]) & (segment[:, None] == segment[None, :])
    scores = jnp.where(allowed, scores, -1e30)
    highest = jnp.max(scores, axis=-1, keepdims=True)
    exponent = jnp.exp(scores - highest)
    return (exponent / jnp.sum(exponent, axis=-1, keepdims=True)).astype(jnp.bfloat16)


def dequantize(code_rows, scale_rows):
    rows_here = code_rows.shape[0]
    kv_heads = scale_rows.shape[1]
    head_dim = code_rows.shape[1] // kv_heads
    scaled = (
        code_rows.astype(jnp.float32).reshape(rows_here, kv_heads, head_dim)
        * scale_rows[:, :, None]
    )
    return scaled.reshape(rows_here, code_rows.shape[1]).astype(jnp.bfloat16)


def local(activations, queries, keys, segment_ids, cotangent, value_codes, value_scales):
    tokens_here = activations.shape[0]
    kv_heads = value_scales.shape[1]
    value_width = value_codes.shape[1]
    head_dim = value_width // kv_heads
    group = queries.shape[1] // value_width
    probability = attention_weights(queries, keys, segment_ids[0], kv_heads, head_dim)
    code_rows = lax.all_gather(value_codes, ("node", "cross"), axis=0, tiled=True)
    scale_rows = lax.all_gather(
        value_scales.astype(jnp.bfloat16), ("node", "cross"), axis=0, tiled=True
    ).astype(jnp.float32)
    columns = activations
    values_f32 = jnp.dot(
        columns, dequantize(code_rows, scale_rows), preferred_element_type=jnp.float32
    )
    values = values_f32.astype(jnp.bfloat16).reshape(tokens_here, kv_heads, head_dim)
    attended = jnp.einsum("gcts,sgd->tgcd", probability, values, preferred_element_type=jnp.float32)
    attended = attended.reshape(tokens_here, queries.shape[1]).astype(jnp.bfloat16)
    grad_rows = cotangent.reshape(tokens_here, kv_heads, group, head_dim)
    dvalue = jnp.einsum(
        "gcts,tgcd->sgd", probability, grad_rows, preferred_element_type=jnp.float32
    )
    dvalue = dvalue.reshape(tokens_here, value_width).astype(jnp.bfloat16)
    factor = 1.0 / math.sqrt(tokens_here * lax.axis_size("node") * lax.axis_size("cross"))
    columns = activations
    product = lax.dot_general(
        columns, dvalue, (((0,), (0,)), ((), ())), preferred_element_type=jnp.float32
    )
    weight_grad = lax.psum_scatter(
        product * factor, ("node", "cross"), scatter_dimension=0, tiled=True
    )
    return (attended, weight_grad)


def solution(mesh):
    in_specs = (
        P(("node", "cross"), None),
        P(("node", "cross"), None),
        P(("node", "cross"), None),
        P(("node", "cross"), None),
        P(("node", "cross"), None),
        P(("node", "cross"), None),
        P(("node", "cross"), None),
    )
    out_specs = (P(("node", "cross"), None), P(("node", "cross"), None))
    return jax.shard_map(local, mesh=mesh, in_specs=in_specs, out_specs=out_specs, check_vma=False)
```

profile of v0, /device:TPU:1, one launch (start us, length us, event | category | flops | bytes accessed | tf_op | source)
XLA Modules:
  0.0 2005.8 jit_solution(7549020687441420611)
XLA Ops:
  7.2 0.0 copy-start.5
  7.2 0.0 all-gather.3.cloned.1.call-start
  7.2 0.7 all-gather.3.cloned.1.call-update
  7.9 0.0 reduce-scatter.4.cloned.1.call-start
  8.0 1.0 reshape.28
  9.0 2.1 copy.57
  11.0 4.1 copy.52
  15.1 0.0 copy-done.5
  15.1 0.1 fusion.15
  15.2 1.4 fusion.8
  16.6 2.4 fusion.18
  19.0 0.0 copy-start.4
  19.0 0.0 copy-start.2
  19.0 1.1 divide_convert_fusion
  20.1 0.0 copy-start
  20.1 2.1 copy-done
  22.2 0.0 copy-done.4
  22.3 1.5 fusion.13
  23.7 8.1 multiply_bitcast_fusion
  31.8 17.5 copy.53
  49.3 0.0 reduce-scatter.4.cloned.1.call-update
  49.3 0.7 copy-done.6
  50.0 597.5 %all-gather = bf16[256,32,4]{1,2,0:T(4,128)(2,1)S(1)} all-gather(bf16[1,32,4]{1,2,0:T(4,128)(2,1)S(1)} %convert_bitcast_fusion), channel_id=1, replica_groups=mesh['node'=16,'cross'=16] {'node','cross'}, dimensions={0}, use_global_device_ids=true | all-gather | bytes 65792 | tf_op jit(solution)/shard_map/all_gather | solution.py:44
  647.5 0.1 copy.34
  647.6 4.3 copy.49
  651.9 79.9 %all-gather.3.cloned.1.call-done = bf16[8192,512]{1,0:T(8,128)(2,1)} async-done(((bf16[32,512]{1,0:T(8,128)(2,1)}), bf16[8192,512]{1,0:T(8,128)(2,1)}) %all-gather.3.cloned.1.call-update) | async-done | bytes 8388624 | tf_op jit(solution)/shard_map/all_gather | solution.py:43
  731.8 16.8 mul.20
  748.6 0.0 copy-done.3
  748.6 13.1 fusion.10
  761.7 0.7 convolution_convert_fusion
  762.4 2.9 copy.42
  765.3 1233.6 %reduce-scatter.4.cloned.1.call-done = f32[32,512]{1,0:T(8,128)} async-done(((f32[8192,512]{1,0:T(8,128)}), f32[32,512]{1,0:T(8,128)}) %reduce-scatter.4.cloned.1.call-update) | async-done | bytes 65552
  (6 shorter events, 0.0 us)
Async XLA Ops:
  7.2 8.0 copy-start.5
  7.2 724.6 %all-gather.3.cloned.1.call-start = ((), (), s32[]{:S(2)}) async-start(), calls=%async_computation.1 | async-start | bytes 8421376 | tf_op jit(solution)/shard_map/all_gather | solution.py:43
  7.9 1991.0 %reduce-scatter.4.cloned.1.call-start = ((), (), s32[]{:S(2)}) async-start(), calls=%async_computation.2 | async-start | bytes 16842752
  19.0 3.3 copy-start.4
  19.0 4.8 copy-start.2
  20.1 2.1 copy-start
  49.3 0.7 copy-start.6
  731.8 16.8 copy-start.3
  748.6 13.1 copy-start.1
Sparse Core Ops, SparseCore 0:
  9.9 721.8 all-gather.2
  734.9 1263.9 reduce-scatter.3
where the time goes:
time: 2040 us; the launch traced here: 2010 us
  waiting for transfers between devices  1310 us (64%)
  blocking collectives  597 us (29%)
  local copies, waits for them, and re-layouts  51.5 us (3%)
  matrix products  24.7 us (1%)
    unnamed x3, waiting for transfers between devices  1230 us
    all_gather x1, blocking collectives, local(): lax.all_gather(value_scales.astype(jnp.bfloat16), ('node', 'cross'), axis...  597 us
    all_gather x1, waiting for transfers between devices, local(): lax.all_gather(value_codes, ('node', 'cross'), axis=0, tiled=True)  79.9 us
  transfers between devices with their start and end apart: 2, of which 2 were waited for; matrix products, arithmetic and copies ran while one was open for 4% of the time, Pallas kernels for 0%

commit v1 on v0

v1 whole, which is shorter than its diff:
```python
import functools
import math

import jax
import jax.numpy as jnp
from jax import lax
from jax.experimental import pallas as pl
from jax.experimental.pallas import tpu as pltpu
from jax.sharding import Mesh, PartitionSpec as P

NY, NX, NC, NZ = 4, 4, 2, 8
AXES = ("y", "xh", "c", "xl", "z")
BF, F32 = jnp.bfloat16, jnp.float32
MIB = 1024 * 1024


def swap_cores(array):
    return lax.ppermute(array, "c", [(0, 1), (1, 0)])


def params(mib=20):
    return pltpu.CompilerParams(vmem_limit_bytes=mib * MIB)


def pick_kernel(place, act_ref, out_ref, sems):
    blocks = out_ref.shape[1] // 512
    copies = []
    for i in range(blocks):
        at = pl.multiple_of(i * 1024 + (1 - place[0]) * 512, 512)
        copies.append(
            pltpu.make_async_copy(
                act_ref.at[:, pl.ds(at, 512)], out_ref.at[:, pl.ds(i * 512, 512)], sems.at[i]
            )
        )
    for copy in copies:
        copy.start()
    for copy in copies:
        copy.wait()


def other_half(place, activations):
    tokens, width = activations.shape
    return pl.pallas_call(
        pick_kernel,
        out_shape=jax.ShapeDtypeStruct((tokens, width // 2), BF),
        in_specs=[pl.BlockSpec(memory_space=pltpu.SMEM), pl.BlockSpec(memory_space=pltpu.HBM)],
        out_specs=pl.BlockSpec(memory_space=pltpu.VMEM),
        scratch_shapes=[pltpu.SemaphoreType.DMA((width // 1024,))],
        compiler_params=params(60),
        cost_estimate=pl.CostEstimate(flops=0, bytes_accessed=2 * tokens * width, transcendentals=0),
        name="other_half",
    )(place, activations)


def copies_of(pairs, sems):
    return [pltpu.make_async_copy(a, b, sems.at[i]) for i, (a, b) in enumerate(pairs)]


def start(copies):
    for copy in copies:
        copy.start()


def columns(ref, i, width):
    return ref.at[:, pl.ds(i * width, width)]


def weights_kernel(head_dim, q_ref, k_ref, cot_ref, segment_ref, p_ref, dv_ref):
    length = q_ref.shape[0]
    kv_heads = k_ref.shape[1] // head_dim
    group = q_ref.shape[1] // k_ref.shape[1]
    row = segment_ref[...]
    column = jnp.broadcast_to(row.astype(F32), (128, length)).T[:, :1].astype(jnp.int32)
    u = lax.broadcasted_iota(jnp.int32, (length, length), 0)
    t = lax.broadcasted_iota(jnp.int32, (length, length), 1)
    bias = jnp.where((u <= t) & (column == row), 0.0, -1e30)
    rate = math.log2(math.e) / math.sqrt(head_dim)
    for g in range(kv_heads):
        total = jnp.zeros((length, head_dim), F32)
        own = slice(g * head_dim, (g + 1) * head_dim)
        for h in range(g * group, (g + 1) * group):
            cols = slice(h * head_dim, (h + 1) * head_dim)
            scores = lax.dot_general(
                k_ref[:, own], q_ref[:, cols], (((1,), (1,)), ((), ())), preferred_element_type=F32
            )
            scores = scores + bias
            highest = jnp.max(scores, axis=0, keepdims=True)
            exponent = jnp.exp2((scores - highest) * rate)
            share = 1.0 / jnp.sum(exponent, axis=0, keepdims=True)
            probability = (exponent * share).astype(BF)
            p_ref[h] = probability
            total = total + jnp.dot(probability, cot_ref[:, cols], preferred_element_type=F32)
        dv_ref[:, own] = total.astype(BF)


INSIDE = pl.BlockSpec(memory_space=pltpu.VMEM)
OUTSIDE = pl.BlockSpec(memory_space=pl.ANY)
HBM = pl.BlockSpec(memory_space=pltpu.HBM)
SCALARS = pl.BlockSpec(memory_space=pltpu.SMEM)


def cost(flops, mib, exps=0):
    return pl.CostEstimate(flops=flops, bytes_accessed=mib * MIB, transcendentals=exps)


def attention_weights(queries, keys, segment_ids, cotangent, kv_heads):
    length, width = queries.shape
    head_dim = keys.shape[1] // kv_heads
    heads = width // head_dim
    return pl.pallas_call(
        functools.partial(weights_kernel, head_dim),
        out_shape=(
            jax.ShapeDtypeStruct((heads, length, length), BF),
            jax.ShapeDtypeStruct(keys.shape, BF),
        ),
        in_specs=[INSIDE] * 4,
        out_specs=(INSIDE, INSIDE),
        compiler_params=params(),
        cost_estimate=cost(4 * width * length * length, 16, heads * length * length),
        name="attention_weights",
    )(queries, keys, cotangent, segment_ids)


def product_kernel(factor, place, own_ref, got_ref, dvo_ref, dvg_ref, *outs):
    c, y, x = place[0], place[2], place[3]
    dv_own = dvo_ref[...].astype(F32).T.astype(BF)
    dv_got = dvg_ref[...].astype(F32).T.astype(BF)
    for k in (1, 2, 3, 0):
        for m in range(4):
            ty = jnp.where(c == 0, (y + k) % 4, m)
            tx = jnp.where(c == 0, m, (x + k) % 4)
            at_own = pl.multiple_of((ty * 2 + tx // 2) * 1024 + c * 512 + (tx % 2) * 256, 256)
            at_got = pl.multiple_of((ty * 4 + tx) * 256, 256)
            rows = jnp.dot(
                dv_own, own_ref[:, pl.ds(at_own, 256)], preferred_element_type=F32
            ) + jnp.dot(dv_got, got_ref[:, pl.ds(at_got, 256)], preferred_element_type=F32)
            outs[k][m] = (rows * factor).astype(BF)


def product(place, act_own, act_got, dv_own, dv_got, factor):
    tokens, width = act_own.shape
    wide = dv_own.shape[1]
    return pl.pallas_call(
        functools.partial(product_kernel, factor),
        out_shape=(jax.ShapeDtypeStruct((4, wide, 256), BF),) * 4,
        in_specs=[SCALARS] + [INSIDE] * 4,
        out_specs=(INSIDE,) * 4,
        compiler_params=params(),
        cost_estimate=cost(2 * tokens * width * wide, 12),
        name="product",
    )(place, act_own, act_got, dv_own, dv_got)


def values_kernel(place, own_ref, got_ref, *refs):
    pieces, (vo_ref, vg_ref, weight, sw) = refs[: NZ + 1], refs[NZ + 1 :]
    rows, wide = pieces[0].shape[1:]
    c = place[0]
    places = weight.shape[0]
    spans = [(0, 0, places), (-1, 0, places), (1, 0, places), (-2, 0, places), (2, 0, places)]
    spans += [(-3, 0, places), (3, 0, places), (4, 0, places // 2), (4, places // 2, places // 2)]
    pairs = []
    for piece, (k, low, count) in zip(pieces, spans):
        z = (place[1] + k + NZ) % NZ
        at = pl.ds(pl.multiple_of(z * rows, rows), rows)
        pairs.append((piece, weight.at[pl.ds(low, count), at]))
    incoming = copies_of(pairs, sw)
    start(incoming)
    for copy in incoming:
        copy.wait()
    own = got = None
    for i in range(places // 2):
        at = pl.multiple_of(i * 1024 + c * 512, 512)
        block = weight[pl.ds(2 * i, 2)].reshape(512, wide)
        left = jnp.dot(own_ref[:, pl.ds(at, 512)], block, preferred_element_type=F32)
        right = jnp.dot(got_ref[:, i * 512 : (i + 1) * 512], block, preferred_element_type=F32)
        own, got = (left, right) if i == 0 else (own + left, got + right)
    vo_ref[...] = own
    vg_ref[...] = got


def partial_values(place, act_own, act_got, pieces):
    tokens, width = act_own.shape
    places, rows, wide = pieces[0].shape
    return pl.pallas_call(
        values_kernel,
        out_shape=(jax.ShapeDtypeStruct((tokens, wide), F32),) * 2,
        in_specs=[SCALARS, INSIDE, INSIDE] + [OUTSIDE] * (1 + NZ),
        out_specs=(INSIDE, INSIDE),
        scratch_shapes=[
            pltpu.VMEM((places, NZ * rows, wide), BF),
            pltpu.SemaphoreType.DMA((NZ + 1,)),
        ],
        compiler_params=params(),
        cost_estimate=cost(2 * tokens * width * wide, 12),
        name="partial_values",
    )(place, act_own, act_got, *pieces)


def add_kernel(place, *refs):
    sources, outs = refs[:4], refs[4:]
    near = jnp.where(place[0] == 0, place[3], place[2])
    for j in (1, 2, 3, 0):
        at = (near + j) % 4
        total = sources[0][at].astype(F32)
        for source in sources[1:]:
            total = total + source[at].astype(F32)
        outs[j][...] = total.astype(BF)


def add_far(place, parts):
    _, wide, rows = parts[0].shape
    return pl.pallas_call(
        add_kernel,
        out_shape=(jax.ShapeDtypeStruct((wide, rows), BF),) * 4,
        in_specs=[SCALARS] + [INSIDE] * 4,
        out_specs=(INSIDE,) * 4,
        compiler_params=params(),
        cost_estimate=cost(16 * rows * wide, 5),
        name="add_far",
    )(place, *parts)


def near_kernel(place, *refs):
    sources, (keep_ref, send_ref, rows) = refs[:4], refs[4:]
    total = sources[0][...].astype(F32)
    for ref in sources[1:]:
        total = total + ref[...].astype(F32)
    rows[...] = total.T
    low = place[1] % 2
    for i in range(4):
        keep = pl.ds(pl.multiple_of((2 * i + low) * 32, 32), 32)
        send = pl.ds(pl.multiple_of((2 * i + 1 - low) * 32, 32), 32)
        keep_ref[i] = rows[keep, :]
        send_ref[i] = rows[send, :].astype(BF)


def add_near(place, parts):
    wide, rows = parts[0].shape
    return pl.pallas_call(
        near_kernel,
        out_shape=(
            jax.ShapeDtypeStruct((4, 32, wide), F32),
            jax.ShapeDtypeStruct((4, 32, wide), BF),
        ),
        in_specs=[SCALARS] + [INSIDE] * 4,
        out_specs=(INSIDE, INSIDE),
        scratch_shapes=[pltpu.VMEM((rows, wide), F32)],
        compiler_params=params(),
        cost_estimate=cost(4 * rows * wide, 2),
        name="add_near",
    )(place, *parts)


def pair_kernel(place, keep_ref, got_ref, *outs):
    for j in range(4):
        at = (place[1] // 2 + j) % 4
        total = keep_ref[at] + got_ref[at].astype(F32)
        outs[j][...] = total.astype(outs[j].dtype)


def add_pair(place, keep, got):
    shape = keep.shape[1:]
    return pl.pallas_call(
        pair_kernel,
        out_shape=tuple(jax.ShapeDtypeStruct(shape, BF if j else F32) for j in range(4)),
        in_specs=[SCALARS, INSIDE, INSIDE],
        out_specs=(INSIDE,) * 4,
        compiler_params=params(),
        cost_estimate=cost(keep.size, 1),
        name="add_pair",
    )(place, keep, got)


def attend_kernel(head_dim, p_hbm, vo_ref, vg_ref, out_hbm, p, out, si, so):
    kv_heads, length, wide = out.shape
    group = wide // head_dim
    incoming = copies_of([(p_hbm.at[pl.ds(g * group, group)], p.at[g]) for g in range(kv_heads)], si)
    outgoing = copies_of([(out.at[g], columns(out_hbm, g, wide)) for g in range(kv_heads)], so)
    start(incoming)
    for g in range(kv_heads):
        own = slice(g * head_dim, (g + 1) * head_dim)
        values = (vo_ref[:, own] + vg_ref[:, own]).astype(BF)
        incoming[g].wait()
        for h in range(group):
            out[g, :, h * head_dim : (h + 1) * head_dim] = lax.dot_general(
                p[g, h], values, (((0,), (0,)), ((), ())), preferred_element_type=F32
            ).astype(BF)
        outgoing[g].start()
    for copy in outgoing:
        copy.wait()


def attend(probability, values_own, values_got, kv_heads):
    heads, length, _ = probability.shape
    head_dim = values_own.shape[1] // kv_heads
    group = heads // kv_heads
    return pl.pallas_call(
        functools.partial(attend_kernel, head_dim),
        out_shape=jax.ShapeDtypeStruct((length, heads * head_dim), BF),
        in_specs=[OUTSIDE, INSIDE, INSIDE],
        out_specs=OUTSIDE,
        scratch_shapes=[
            pltpu.VMEM((kv_heads, group, length, length), BF),
            pltpu.VMEM((kv_heads, length, group * head_dim), BF),
            pltpu.SemaphoreType.DMA((kv_heads,)),
            pltpu.SemaphoreType.DMA((kv_heads,)),
        ],
        compiler_params=params(),
        cost_estimate=cost(2 * heads * head_dim * length * length, 8),
        name="attend",
    )(probability, values_own, values_got)


PLANE = ("y", "xh", "xl")


def exchange(array, axes):
    return lax.all_to_all(array, axes, 0, 0, tiled=True)


def along_z(array, k):
    return lax.ppermute(array, "z", [(z, (z + k) % NZ) for z in range(NZ)])


def gather_near(weight):
    rows, wide = weight.shape
    places = NY * NX
    return exchange(jnp.tile(weight, (places, 1)), PLANE).reshape(places, rows, wide)


def gather_first(near):
    return along_z(near, 1), along_z(near, -1)


def gather_rest(near, up, down, product_part, far_sum):
    pieces = [near, up, down]
    up, down = after(up, product_part), after(down, product_part)
    for _ in range(2):
        up, down = along_z(up, 1), along_z(down, -1)
        pieces += [up, down]
    half = near.shape[0] // 2
    up, down = after(up, far_sum), after(down, far_sum)
    return pieces + [along_z(up[:half], 1), along_z(down[half:], -1)]


def along(array, k, far):
    pairs = []
    for y in range(NY):
        for x in range(NX):
            for c in range(NC):
                ty, tx = ((y + k) % NY, x) if far == (c == 0) else (y, (x + k) % NX)
                for z in range(NZ):
                    source = (((y * 2 + x // 2) * 2 + c) * 2 + x % 2) * NZ + z
                    target = (((ty * 2 + tx // 2) * 2 + c) * 2 + tx % 2) * NZ + z
                    pairs.append((source, target))
    return lax.ppermute(array, AXES, pairs)


def spread(parts, far):
    return [parts[0]] + [along(parts[k], k, far) for k in (1, 2, 3)]


def reduce_last(place, keep, got, attended):
    parts = add_pair(place, keep, got)
    moved = [along_z(parts[j], 2 * j) for j in (1, 2, 3)]
    total = parts[0] + after(moved[0], attended).astype(F32)
    return total + moved[1].astype(F32) + moved[2].astype(F32)


def after(array, other):
    return lax.optimization_barrier((array, other))[0]


def local(activations, queries, keys, segment_ids, cotangent, value_codes, value_scales):
    rows_here, kv_heads = value_scales.shape
    x = lax.axis_index("xh") * 2 + lax.axis_index("xl")
    place = [lax.axis_index("c"), lax.axis_index("z"), lax.axis_index("y"), x]
    place = jnp.stack(place).astype(jnp.int32)
    weight = (
        value_codes.astype(F32).reshape(rows_here, kv_heads, -1) * value_scales[:, :, None]
    ).reshape(rows_here, -1).astype(BF)
    factor = 1.0 / math.sqrt(activations.shape[0] * NY * NX * NC * NZ)
    act_got = swap_cores(other_half(place, activations))
    near = gather_near(weight)
    probability, dvalue = attention_weights(queries, keys, segment_ids, cotangent, kv_heads)
    dv_got = swap_cores(dvalue)
    near = after(near, dv_got)
    up, down = gather_first(near)
    parts = product(place, activations, act_got, dvalue, dv_got, factor)
    far_sums = add_far(place, spread(parts, True))
    pieces = gather_rest(near, up, down, parts[0], far_sums[0])
    keep, send = add_near(place, spread(far_sums, False))
    got = lax.ppermute(send, "z", [(z, z ^ 1) for z in range(NZ)])
    pieces[-1] = after(pieces[-1], send)
    values_own, values_other = partial_values(place, activations, act_got, pieces)
    attended = attend(probability, values_own, swap_cores(values_other), kv_heads)
    return (attended, reduce_last(place, keep, got, attended))


def solution(mesh):
    inner = Mesh(mesh.devices.reshape(NY, 2, NC, 2, NZ), AXES)
    rows = P(AXES, None)
    return jax.shard_map(
        local, mesh=inner, in_specs=(rows,) * 7, out_specs=(rows, rows), check_vma=False
    )
```

time: 2040 us -> 105 us (0.05); the launches traced: 2010 us -> 104 us
  waiting for transfers between devices: 1310 us -> 30.8 us
  blocking collectives: 597 us -> 0 us
  local copies, waits for them, and re-layouts: 51.5 us -> 6.84 us
  starting transfers between devices: 0.08 us -> 41.5 us
  matrix products: 24.7 us -> 0 us
  Pallas kernels: 0 us -> 22.9 us
    unnamed x3 -> x0, waiting for transfers between devices: 1230 us -> none
    all_gather x1 -> x0, blocking collectives: 597 us -> none  [local(): lax.all_gather(value_scales.astype(jnp.bfloat16), ('node', 'cross'), axis...]
    all_gather x1 -> x0, waiting for transfers between devices: 79.9 us -> none  [local(): lax.all_gather(value_codes, ('node', 'cross'), axis=0, tiled=True)]
    ppermute x0 -> x21, starting transfers between devices: none -> 36.5 us  [the longest x11 19.9 us: along_z(): return lax.ppermute(array, 'z', [(z, (z + k) % NZ) for z in range(NZ)])]
    ppermute x0 -> x21, waiting for transfers between devices: none -> 29.9 us  [the longest x6 11.9 us: along(): return lax.ppermute(array, AXES, pairs)]
    dot_general x5 -> x0, matrix products: 24.7 us -> none  [the longest x1 13.1 us: local(): jnp.dot(columns, dequantize(code_rows, scale_rows), preferred_element_typ...]
    pallas_call x0 -> x8, Pallas kernels: none -> 22.9 us  [the longest x1 5.05 us: attention_weights(): pl.pallas_call(functools.partial(weights_kernel, head_dim), out_shape=(ja...]
  transfers between devices with their start and end apart: 2 -> 22, of which waited for: 2 -> 8; matrix products, arithmetic and copies ran while one was open for 4% -> 1% of each run, Pallas kernels for 0% -> 14%
where the time goes in v1:
time: 105 us; the launch traced here: 104 us
  starting transfers between devices  41.5 us (40%)
  waiting for transfers between devices  30.8 us (29%)
  Pallas kernels  22.9 us (22%)
  local copies, waits for them, and re-layouts  6.84 us (7%)
  other arithmetic  1.31 us (1%)
    ppermute x11, starting transfers between devices, along_z(): return lax.ppermute(array, 'z', [(z, (z + k) % NZ) for z in range(NZ)])  19.9 us
    ppermute x6, waiting for transfers between devices, along(): return lax.ppermute(array, AXES, pairs)  11.9 us
    ppermute x11, waiting for transfers between devices, along_z(): return lax.ppermute(array, 'z', [(z, (z + k) % NZ) for z in range(NZ)])  11.7 us
    ppermute x6, starting transfers between devices, along(): return lax.ppermute(array, AXES, pairs)  8.61 us
    ppermute x3, starting transfers between devices, swap_cores(): return lax.ppermute(array, 'c', [(0, 1), (1, 0)])  8.05 us
    unnamed x23, local copies, waits for them, and re-layouts  5.86 us
    ppermute x1, waiting for transfers between devices, local(): got = lax.ppermute(send, 'z', [(z, z ^ 1) for z in range(NZ)])  5.06 us
    pallas_call x1, Pallas kernels, attention_weights(): pl.pallas_call(functools.partial(weights_kernel, head_dim), out_shape=(ja...  5.05 us
  transfers between devices with their start and end apart: 22, of which 8 were waited for; matrix products, arithmetic and copies ran while one was open for 1% of the time, Pallas kernels for 14%

profile of v1, /device:TPU:1, one launch (start us, length us, event | category | flops | bytes accessed | tf_op | source)
XLA Modules:
  0.0 104.3 jit_solution(2531060441917343041)
XLA Ops:
  1.3 3.7 %other_half.1 = bf16[256,4096]{1,0:T(8,128)(2,1)} custom-call(s32[4]{0:T(128)} %pad_add_fusion.place, bf16[256,8192]{1,0:T(8,128)(2,1)} %own_ref.3), custom_call_target="tpu_custom_call" | custom-call | bytes 4194304 | tf_op jit(solution)/shard_map/other_half/pallas_call | solution.py:43
  5.0 3.3 %collective-permute-start = (bf16[256,4096]{1,0:T(8,128)(2,1)}, bf16[256,4096]{1,0:T(8,128)(2,1)}, u32[]{:S(2)}, u32[]{:S(2)}) collective-permute-start(bf16[256,4096]{1,0:T(8,128)(2,1)} %other_half.1), channel_id=1, source_target_pairs={{0,16},{16,0},{1,17},{17,1},{2,18},{18,2},{3,19},{19,3},{4,20},{20... | collective-permute-start | bytes 6291464 | tf_op jit(solution)/shard_map/ppermute | solution.py:18
  8.6 0.8 tile.2
  9.4 5.0 %all-to-all-start = ((bf16[16,32,512]{2,1,0:T(8,128)(2,1)}), bf16[16,32,512]{2,1,0:T(8,128)(2,1)S(1)}, u32[]{:S(2)}, u32[]{:S(2)}) async-start(bf16[16,32,512]{2,1,0:T(8,128)(2,1)} %tile.2), calls=%async_computation | async-start | bytes 1048576 | tf_op jit(solution)/shard_map/all_to_all | solution.py:318
  14.5 1.6 %copy-done.5 = bf16[256,4096]{1,0:T(8,128)(2,1)S(1)} copy-done((bf16[256,4096]{1,0:T(8,128)(2,1)S(1)}, bf16[256,4096]{1,0:T(8,128)(2,1)}, u32[]{:S(2)}) %copy-start.5) | copy-done | bytes 2097176
  16.1 5.1 %attention_weights.1 = (bf16[32,256,256]{2,1,0:T(8,128)(2,1)S(1)}, bf16[256,512]{1,0:T(8,128)(2,1)S(1)}) custom-call(bf16[256,4096]{1,0:T(8,128)(2,1)S(1)} %copy-done.4, bf16[256,512]{1,0:T(8,128)(2,1)S(1)} %copy-done.6, bf16[256,4096]{1,0:T(8,128)(2,1)S(1)} %copy-done.5, s32[1,256]{1,0:T(1,128)S(1)} %copy-done.8), custom_call_target="tpu_custom_call" | custom-call | flops 1073741824 | bytes 16777216 | tf_op jit(solution)/shard_map/attention_weights/pallas_call | solution.py:110
  21.1 2.0 %copy-done.2 = bf16[32,256,256]{2,1,0:T(8,128)(2,1)} copy-done((bf16[32,256,256]{2,1,0:T(8,128)(2,1)}, bf16[32,256,256]{2,1,0:T(8,128)(2,1)S(1)}, u32[]{:S(2)}) %copy-start.2) | copy-done | bytes 4194328
  23.4 1.2 %collective-permute-done.1.dvg_ref = bf16[256,512]{1,0:T(8,128)(2,1)S(1)} collective-permute-done((bf16[256,512]{1,0:T(8,128)(2,1)S(1)}, bf16[256,512]{1,0:T(8,128)(2,1)S(1)}, u32[]{:S(2)}, u32[]{:S(2)}) %collective-permute-start.1) | collective-permute-done | bytes 262176 | tf_op jit(solution)/shard_map/ppermute | solution.py:18
  24.7 0.9 all-to-all-done.refs_0_
  25.5 5.6 %collective-permute-start.3 = (bf16[16,32,512]{2,1,0:T(8,128)(2,1)S(1)}, bf16[16,32,512]{2,1,0:T(8,128)(2,1)S(1)}, u32[]{:S(2)}, u32[]{:S(2)}) collective-permute-start(bf16[16,32,512]{2,1,0:T(8,128)(2,1)S(1)} %all-to-all-done.refs_0_), channel_id=1, source_target_pairs={{0,7},{1,0},{2,1},{3,2},{4,3},{5,4},{6,5},{7,6},{8,15},{9,8},{10,9... | collective-permute-start | bytes 1572872 | tf_op jit(solution)/shard_map/ppermute | solution.py:322
  31.1 2.2 %copy-done = bf16[256,8192]{1,0:T(8,128)(2,1)S(1)} copy-done((bf16[256,8192]{1,0:T(8,128)(2,1)S(1)}, bf16[256,8192]{1,0:T(8,128)(2,1)}, u32[]{:S(2)}) %copy-start) | copy-done | bytes 4194328
  33.3 4.0 %product.1 = (bf16[4,512,256]{2,1,0:T(8,128)(2,1)S(1)}, bf16[4,512,256]{2,1,0:T(8,128)(2,1)S(1)}, bf16[4,512,256]{2,1,0:T(8,128)(2,1)S(1)}, bf16[4,512,256]{2,1,0:T(8,128)(2,1)S(1)}) custom-call(s32[4]{0:T(128)S(1)} %copy-done.7, bf16[256,8192]{1,0:T(8,128)(2,1)S(1)} %copy-done, bf16[256,4096]{1,0:T(8,128)(2,1)} %collective-permute-done.got_ref, ...), custom_call_target="tpu_custom_call" | custom-call | flops 2147483648 | bytes 12582912 | tf_op jit(solution)/shard_map/product/pallas_call | solution.py:143
  37.3 2.0 %collective-permute-start.10 = (bf16[4,512,256]{2,1,0:T(8,128)(2,1)S(1)}, bf16[4,512,256]{2,1,0:T(8,128)(2,1)S(1)}, u32[]{:S(2)}, u32[]{:S(2)}) collective-permute-start(bf16[4,512,256]{2,1,0:T(8,128)(2,1)S(1)} %get-tuple-element.35), channel_id=1, source_target_pairs={{0,192},{1,193},{2,194},{3,195},{4,196},{5,197},{6,198},{7,199},{1... | collective-permute-start | bytes 3145736 | tf_op jit(solution)/shard_map/ppermute | solution.py:356
  39.3 1.8 %collective-permute-start.9 = (bf16[4,512,256]{2,1,0:T(8,128)(2,1)S(1)}, bf16[4,512,256]{2,1,0:T(8,128)(2,1)S(1)}, u32[]{:S(2)}, u32[]{:S(2)}) collective-permute-start(bf16[4,512,256]{2,1,0:T(8,128)(2,1)S(1)} %get-tuple-element.34), channel_id=1, source_target_pairs={{0,128},{1,129},{2,130},{3,131},{4,132},{5,133},{6,134},{7,135},{1... | collective-permute-start | bytes 3145736 | tf_op jit(solution)/shard_map/ppermute | solution.py:356
  41.1 3.2 %collective-permute-start.5 = (bf16[16,32,512]{2,1,0:T(8,128)(2,1)S(1)}, bf16[16,32,512]{2,1,0:T(8,128)(2,1)S(1)}, u32[]{:S(2)}, u32[]{:S(2)}) collective-permute-start(bf16[16,32,512]{2,1,0:T(8,128)(2,1)S(1)} %collective-permute-done.3.refs_2_), channel_id=1, source_target_pairs={{0,7},{1,0},{2,1},{3,2},{4,3},{5,4},{6,5},{7,6},{8,15},{9,8},{10,9... | collective-permute-start | bytes 1572872 | tf_op jit(solution)/shard_map/ppermute | solution.py:322
  44.3 8.9 %collective-permute-done.5.refs_4_ = bf16[16,32,512]{2,1,0:T(8,128)(2,1)S(1)} collective-permute-done((bf16[16,32,512]{2,1,0:T(8,128)(2,1)S(1)}, bf16[16,32,512]{2,1,0:T(8,128)(2,1)S(1)}, u32[]{:S(2)}, u32[]{:S(2)}) %collective-permute-start.5) | collective-permute-done | bytes 524320 | tf_op jit(solution)/shard_map/ppermute | solution.py:322
  53.2 3.4 %collective-permute-start.7 = (bf16[16,32,512]{2,1,0:T(8,128)(2,1)S(1)}, bf16[16,32,512]{2,1,0:T(8,128)(2,1)S(1)}, u32[]{:S(2)}, u32[]{:S(2)}) collective-permute-start(bf16[16,32,512]{2,1,0:T(8,128)(2,1)S(1)} %collective-permute-done.5.refs_4_), channel_id=1, source_target_pairs={{0,7},{1,0},{2,1},{3,2},{4,3},{5,4},{6,5},{7,6},{8,15},{9,8},{10,9... | collective-permute-start | bytes 1572872 | tf_op jit(solution)/shard_map/ppermute | solution.py:322
  56.6 5.7 %collective-permute-done.10.refs_3_ = bf16[4,512,256]{2,1,0:T(8,128)(2,1)S(1)} collective-permute-done((bf16[4,512,256]{2,1,0:T(8,128)(2,1)S(1)}, bf16[4,512,256]{2,1,0:T(8,128)(2,1)S(1)}, u32[]{:S(2)}, u32[]{:S(2)}) %collective-permute-start.10) | collective-permute-done | bytes 1048608 | tf_op jit(solution)/shard_map/ppermute | solution.py:356
  62.3 3.4 %collective-permute-done.8.refs_1_ = bf16[4,512,256]{2,1,0:T(8,128)(2,1)S(1)} collective-permute-done((bf16[4,512,256]{2,1,0:T(8,128)(2,1)S(1)}, bf16[4,512,256]{2,1,0:T(8,128)(2,1)S(1)}, u32[]{:S(2)}, u32[]{:S(2)}) %collective-permute-start.8) | collective-permute-done | bytes 1048608 | tf_op jit(solution)/shard_map/ppermute | solution.py:356
  65.7 1.1 %add_far.1 = (bf16[512,256]{1,0:T(8,128)(2,1)S(1)}, bf16[512,256]{1,0:T(8,128)(2,1)S(1)}, bf16[512,256]{1,0:T(8,128)(2,1)S(1)}, bf16[512,256]{1,0:T(8,128)(2,1)S(1)}) custom-call(s32[4]{0:T(128)S(1)} %copy-done.7, bf16[4,512,256]{2,1,0:T(8,128)(2,1)S(1)} %get-tuple-element.30.refs_0_, bf16[4,512,256]{2,1,0:T(8,128)(2,1)S(1)} %collective-permute-done.8.refs_1_, ...), custom_call_target="tpu_custom_call" | custom-call | flops 2097152 | bytes 5242880 | tf_op jit(solution)/shard_map/add_far/pallas_call | solution.py:212
  66.8 1.3 %collective-permute-start.13 = (bf16[512,256]{1,0:T(8,128)(2,1)S(1)}, bf16[512,256]{1,0:T(8,128)(2,1)S(1)}, u32[]{:S(2)}, u32[]{:S(2)}) collective-permute-start(bf16[512,256]{1,0:T(8,128)(2,1)S(1)} %get-tuple-element.39), channel_id=1, source_target_pairs={{0,8},{1,9},{2,10},{3,11},{4,12},{5,13},{6,14},{7,15},{16,80},{17,... | collective-permute-start | bytes 786440 | tf_op jit(solution)/shard_map/ppermute | solution.py:356
  68.0 2.4 %collective-permute-start.14 = (bf16[512,256]{1,0:T(8,128)(2,1)S(1)}, bf16[512,256]{1,0:T(8,128)(2,1)S(1)}, u32[]{:S(2)}, u32[]{:S(2)}) collective-permute-start(bf16[512,256]{1,0:T(8,128)(2,1)S(1)} %get-tuple-element.40), channel_id=1, source_target_pairs={{0,32},{1,33},{2,34},{3,35},{4,36},{5,37},{6,38},{7,39},{16,144},{... | collective-permute-start | bytes 786440 | tf_op jit(solution)/shard_map/ppermute | solution.py:356
  70.4 1.2 %collective-permute-start.15 = (bf16[512,256]{1,0:T(8,128)(2,1)S(1)}, bf16[512,256]{1,0:T(8,128)(2,1)S(1)}, u32[]{:S(2)}, u32[]{:S(2)}) collective-permute-start(bf16[512,256]{1,0:T(8,128)(2,1)S(1)} %get-tuple-element.41), channel_id=1, source_target_pairs={{0,40},{1,41},{2,42},{3,43},{4,44},{5,45},{6,46},{7,47},{16,208},{... | collective-permute-start | bytes 786440 | tf_op jit(solution)/shard_map/ppermute | solution.py:356
  71.6 2.7 %collective-permute-start.12 = (bf16[8,32,512]{2,1,0:T(8,128)(2,1)S(1)}, bf16[8,32,512]{2,1,0:T(8,128)(2,1)S(1)}, u32[]{:S(2)}, u32[]{:S(2)}) collective-permute-start(bf16[8,32,512]{2,1,0:T(8,128)(2,1)S(1)} %slice.7), channel_id=1, source_target_pairs={{0,7},{1,0},{2,1},{3,2},{4,3},{5,4},{6,5},{7,6},{8,15},{9,8},{10,9... | collective-permute-start | bytes 786440 | tf_op jit(solution)/shard_map/ppermute | solution.py:322
  74.5 2.8 %collective-permute-done.14.refs_2_ = bf16[512,256]{1,0:T(8,128)(2,1)S(1)} collective-permute-done((bf16[512,256]{1,0:T(8,128)(2,1)S(1)}, bf16[512,256]{1,0:T(8,128)(2,1)S(1)}, u32[]{:S(2)}, u32[]{:S(2)}) %collective-permute-start.14) | collective-permute-done | bytes 262176 | tf_op jit(solution)/shard_map/ppermute | solution.py:356
  78.1 2.8 %collective-permute-done.11.refs_7_ = bf16[8,32,512]{2,1,0:T(8,128)(2,1)S(1)} collective-permute-done((bf16[8,32,512]{2,1,0:T(8,128)(2,1)S(1)}, bf16[8,32,512]{2,1,0:T(8,128)(2,1)S(1)}, u32[]{:S(2)}, u32[]{:S(2)}) %collective-permute-start.11) | collective-permute-done | bytes 262176 | tf_op jit(solution)/shard_map/ppermute | solution.py:322
  80.9 4.5 %partial_values.1 = (f32[256,512]{1,0:T(8,128)S(1)}, f32[256,512]{1,0:T(8,128)S(1)}) custom-call(s32[4]{0:T(128)S(1)} %copy-done.7, bf16[256,8192]{1,0:T(8,128)(2,1)S(1)} %copy-done.1, bf16[256,4096]{1,0:T(8,128)(2,1)} %collective-permute-done.got_ref, bf16[16,32,512]{2,1,0:T(8,128)(2,1)S(1)} %all-to-all-done.refs_0_, ...), custom_call_target="tpu_custom_call" | custom-call | flops 2147483648 | bytes 12582912 | tf_op jit(solution)/shard_map/partial_values/pallas_call | solution.py:184
  85.4 4.4 %collective-permute-start.16 = (f32[256,512]{1,0:T(8,128)S(1)}, f32[256,512]{1,0:T(8,128)S(1)}, u32[]{:S(2)}, u32[]{:S(2)}) collective-permute-start(f32[256,512]{1,0:T(8,128)S(1)} %get-tuple-element.45), channel_id=1, source_target_pairs={{0,16},{16,0},{1,17},{17,1},{2,18},{18,2},{3,19},{19,3},{4,20},{20... | collective-permute-start | bytes 1572872 | tf_op jit(solution)/shard_map/ppermute | solution.py:18
  89.9 5.1 %collective-permute-done.17.got_ref = bf16[4,32,512]{2,1,0:T(8,128)(2,1)S(1)} collective-permute-done((bf16[4,32,512]{2,1,0:T(8,128)(2,1)S(1)}, bf16[4,32,512]{2,1,0:T(8,128)(2,1)S(1)}, u32[]{:S(2)}, u32[]{:S(2)}) %collective-permute-start.17) | collective-permute-done | bytes 131104 | tf_op jit(solution)/shard_map/ppermute | solution.py:393
  95.6 1.6 %collective-permute-start.19 = (bf16[32,512]{1,0:T(8,128)(2,1)S(1)}, bf16[32,512]{1,0:T(8,128)(2,1)S(1)}, u32[]{:S(2)}, u32[]{:S(2)}) collective-permute-start(bf16[32,512]{1,0:T(8,128)(2,1)S(1)} %get-tuple-element.50), channel_id=1, source_target_pairs={{0,4},{1,5},{2,6},{3,7},{4,0},{5,1},{6,2},{7,3},{8,12},{9,13},{10,... | collective-permute-start | bytes 98312 | tf_op jit(solution)/shard_map/ppermute | solution.py:322
  97.2 3.1 %collective-permute-start.20 = (bf16[32,512]{1,0:T(8,128)(2,1)S(1)}, bf16[32,512]{1,0:T(8,128)(2,1)S(1)}, u32[]{:S(2)}, u32[]{:S(2)}) collective-permute-start(bf16[32,512]{1,0:T(8,128)(2,1)S(1)} %get-tuple-element.51), channel_id=1, source_target_pairs={{0,6},{1,7},{2,0},{3,1},{4,2},{5,3},{6,4},{7,5},{8,14},{9,15},{10,... | collective-permute-start | bytes 98312 | tf_op jit(solution)/shard_map/ppermute | solution.py:322
  100.3 3.2 %attend.1 = bf16[256,4096]{1,0:T(8,128)(2,1)} custom-call(bf16[32,256,256]{2,1,0:T(8,128)(2,1)S(1)} %copy-done.3, f32[256,512]{1,0:T(8,128)S(1)} %get-tuple-element.44.vo_ref, f32[256,512]{1,0:T(8,128)S(1)} %collective-permute-done.16.vg_ref), custom_call_target="tpu_custom_call" | custom-call | flops 536870912 | bytes 8388608 | tf_op jit(solution)/shard_map/attend/pallas_call | solution.py:297
  (50 shorter events, 3.5 us)
Async XLA Ops:
  1.3 7.1 %copy-start.10 = (f32[32,4]{0,1:T(4,128)S(1)}, f32[32,4]{0,1:T(4,128)}, u32[]{:S(2)}) copy-start(f32[32,4]{0,1:T(4,128)} %param.13) | copy-start | bytes 1540
  1.3 7.2 %copy-start.9 = (bf16[32,512]{1,0:T(8,128)(2,1)S(1)}, bf16[32,512]{1,0:T(8,128)(2,1)}, u32[]{:S(2)}) copy-start(bf16[32,512]{1,0:T(8,128)(2,1)} %param.12) | copy-start | bytes 98308
  1.3 13.2 %copy-start.4 = (bf16[256,4096]{1,0:T(8,128)(2,1)S(1)}, bf16[256,4096]{1,0:T(8,128)(2,1)}, u32[]{:S(2)}) copy-start(bf16[256,4096]{1,0:T(8,128)(2,1)} %q_ref.1) | copy-start | bytes 6291460
  1.3 13.2 %copy-start.6 = (bf16[256,512]{1,0:T(8,128)(2,1)S(1)}, bf16[256,512]{1,0:T(8,128)(2,1)}, u32[]{:S(2)}) copy-start(bf16[256,512]{1,0:T(8,128)(2,1)} %k_ref.1) | copy-start | bytes 786436
  1.3 13.2 %copy-start.8 = (s32[1,256]{1,0:T(1,128)S(1)}, s32[1,256]{1,0:T(1,128)}, u32[]{:S(2)}) copy-start(s32[1,256]{1,0:T(1,128)} %segment_ref.1) | copy-start | bytes 3076
  5.0 26.1 %collective-permute-start = (bf16[256,4096]{1,0:T(8,128)(2,1)}, bf16[256,4096]{1,0:T(8,128)(2,1)}, u32[]{:S(2)}, u32[]{:S(2)}) collective-permute-start(bf16[256,4096]{1,0:T(8,128)(2,1)} %other_half.1), channel_id=1, source_target_pairs={{0,16},{16,0},{1,17},{17,1},{2,18},{18,2},{3,19},{19,3},{4,20},{20... | collective-permute-start | bytes 6291464 | tf_op jit(solution)/shard_map/ppermute | solution.py:18
  9.4 16.1 %all-to-all-start = ((bf16[16,32,512]{2,1,0:T(8,128)(2,1)}), bf16[16,32,512]{2,1,0:T(8,128)(2,1)S(1)}, u32[]{:S(2)}, u32[]{:S(2)}) async-start(bf16[16,32,512]{2,1,0:T(8,128)(2,1)} %tile.2), calls=%async_computation | async-start | bytes 1048576 | tf_op jit(solution)/shard_map/all_to_all | solution.py:318
  16.1 15.0 %copy-start.7 = (s32[4]{0:T(128)S(1)}, s32[4]{0:T(128)}, u32[]{:S(2)}) copy-start(s32[4]{0:T(128)} %pad_add_fusion.place) | copy-start | bytes 52
  21.1 2.0 %copy-start.2 = (bf16[32,256,256]{2,1,0:T(8,128)(2,1)}, bf16[32,256,256]{2,1,0:T(8,128)(2,1)S(1)}, u32[]{:S(2)}) copy-start(bf16[32,256,256]{2,1,0:T(8,128)(2,1)S(1)} %get-tuple-element.27.p_hbm) | copy-start | bytes 12582916
  23.1 1.5 %collective-permute-start.1 = (bf16[256,512]{1,0:T(8,128)(2,1)S(1)}, bf16[256,512]{1,0:T(8,128)(2,1)S(1)}, u32[]{:S(2)}, u32[]{:S(2)}) collective-permute-start(bf16[256,512]{1,0:T(8,128)(2,1)S(1)} %get-tuple-element.28.dvo_ref), channel_id=1, source_target_pairs={{0,16},{16,0},{1,17},{17,1},{2,18},{18,2},{3,19},{19,3},{4,20},{20... | collective-permute-start | bytes 786440 | tf_op jit(solution)/shard_map/ppermute | solution.py:18
  25.5 15.6 %collective-permute-start.3 = (bf16[16,32,512]{2,1,0:T(8,128)(2,1)S(1)}, bf16[16,32,512]{2,1,0:T(8,128)(2,1)S(1)}, u32[]{:S(2)}, u32[]{:S(2)}) collective-permute-start(bf16[16,32,512]{2,1,0:T(8,128)(2,1)S(1)} %all-to-all-done.refs_0_), channel_id=1, source_target_pairs={{0,7},{1,0},{2,1},{3,2},{4,3},{5,4},{6,5},{7,6},{8,15},{9,8},{10,9... | collective-permute-start | bytes 1572872 | tf_op jit(solution)/shard_map/ppermute | solution.py:322
  31.1 13.2 %collective-permute-start.2 = (bf16[16,32,512]{2,1,0:T(8,128)(2,1)S(1)}, bf16[16,32,512]{2,1,0:T(8,128)(2,1)S(1)}, u32[]{:S(2)}, u32[]{:S(2)}) collective-permute-start(bf16[16,32,512]{2,1,0:T(8,128)(2,1)S(1)} %all-to-all-done.refs_0_), channel_id=1, source_target_pairs={{0,1},{1,2},{2,3},{3,4},{4,5},{5,6},{6,7},{7,0},{8,9},{9,10},{10,1... | collective-permute-start | bytes 1572872 | tf_op jit(solution)/shard_map/ppermute | solution.py:322
  31.1 2.2 %copy-start = (bf16[256,8192]{1,0:T(8,128)(2,1)S(1)}, bf16[256,8192]{1,0:T(8,128)(2,1)}, u32[]{:S(2)}) copy-start(bf16[256,8192]{1,0:T(8,128)(2,1)} %own_ref.3) | copy-start | bytes 12582916
  37.3 25.0 %collective-permute-start.10 = (bf16[4,512,256]{2,1,0:T(8,128)(2,1)S(1)}, bf16[4,512,256]{2,1,0:T(8,128)(2,1)S(1)}, u32[]{:S(2)}, u32[]{:S(2)}) collective-permute-start(bf16[4,512,256]{2,1,0:T(8,128)(2,1)S(1)} %get-tuple-element.35), channel_id=1, source_target_pairs={{0,192},{1,193},{2,194},{3,195},{4,196},{5,197},{6,198},{7,199},{1... | collective-permute-start | bytes 3145736 | tf_op jit(solution)/shard_map/ppermute | solution.py:356
  39.3 26.4 %collective-permute-start.8 = (bf16[4,512,256]{2,1,0:T(8,128)(2,1)S(1)}, bf16[4,512,256]{2,1,0:T(8,128)(2,1)S(1)}, u32[]{:S(2)}, u32[]{:S(2)}) collective-permute-start(bf16[4,512,256]{2,1,0:T(8,128)(2,1)S(1)} %get-tuple-element.33), channel_id=1, source_target_pairs={{0,64},{1,65},{2,66},{3,67},{4,68},{5,69},{6,70},{7,71},{16,24},{1... | collective-permute-start | bytes 3145736 | tf_op jit(solution)/shard_map/ppermute | solution.py:356
  39.3 26.4 %collective-permute-start.9 = (bf16[4,512,256]{2,1,0:T(8,128)(2,1)S(1)}, bf16[4,512,256]{2,1,0:T(8,128)(2,1)S(1)}, u32[]{:S(2)}, u32[]{:S(2)}) collective-permute-start(bf16[4,512,256]{2,1,0:T(8,128)(2,1)S(1)} %get-tuple-element.34), channel_id=1, source_target_pairs={{0,128},{1,129},{2,130},{3,131},{4,132},{5,133},{6,134},{7,135},{1... | collective-permute-start | bytes 3145736 | tf_op jit(solution)/shard_map/ppermute | solution.py:356
  41.1 12.1 %collective-permute-start.5 = (bf16[16,32,512]{2,1,0:T(8,128)(2,1)S(1)}, bf16[16,32,512]{2,1,0:T(8,128)(2,1)S(1)}, u32[]{:S(2)}, u32[]{:S(2)}) collective-permute-start(bf16[16,32,512]{2,1,0:T(8,128)(2,1)S(1)} %collective-permute-done.3.refs_2_), channel_id=1, source_target_pairs={{0,7},{1,0},{2,1},{3,2},{4,3},{5,4},{6,5},{7,6},{8,15},{9,8},{10,9... | collective-permute-start | bytes 1572872 | tf_op jit(solution)/shard_map/ppermute | solution.py:322
  44.3 12.3 %collective-permute-start.4 = (bf16[16,32,512]{2,1,0:T(8,128)(2,1)S(1)}, bf16[16,32,512]{2,1,0:T(8,128)(2,1)S(1)}, u32[]{:S(2)}, u32[]{:S(2)}) collective-permute-start(bf16[16,32,512]{2,1,0:T(8,128)(2,1)S(1)} %collective-permute-done.2.refs_1_), channel_id=1, source_target_pairs={{0,1},{1,2},{2,3},{3,4},{4,5},{5,6},{6,7},{7,0},{8,9},{9,10},{10,1... | collective-permute-start | bytes 1572872 | tf_op jit(solution)/shard_map/ppermute | solution.py:322
  53.2 18.5 %collective-permute-start.7 = (bf16[16,32,512]{2,1,0:T(8,128)(2,1)S(1)}, bf16[16,32,512]{2,1,0:T(8,128)(2,1)S(1)}, u32[]{:S(2)}, u32[]{:S(2)}) collective-permute-start(bf16[16,32,512]{2,1,0:T(8,128)(2,1)S(1)} %collective-permute-done.5.refs_4_), channel_id=1, source_target_pairs={{0,7},{1,0},{2,1},{3,2},{4,3},{5,4},{6,5},{7,6},{8,15},{9,8},{10,9... | collective-permute-start | bytes 1572872 | tf_op jit(solution)/shard_map/ppermute | solution.py:322
  56.6 17.8 %collective-permute-start.6 = (bf16[16,32,512]{2,1,0:T(8,128)(2,1)S(1)}, bf16[16,32,512]{2,1,0:T(8,128)(2,1)S(1)}, u32[]{:S(2)}, u32[]{:S(2)}) collective-permute-start(bf16[16,32,512]{2,1,0:T(8,128)(2,1)S(1)} %collective-permute-done.4.refs_3_), channel_id=1, source_target_pairs={{0,1},{1,2},{2,3},{3,4},{4,5},{5,6},{6,7},{7,0},{8,9},{9,10},{10,1... | collective-permute-start | bytes 1572872 | tf_op jit(solution)/shard_map/ppermute | solution.py:322
  65.7 15.2 %copy-start.1 = (bf16[256,8192]{1,0:T(8,128)(2,1)S(1)}, bf16[256,8192]{1,0:T(8,128)(2,1)}, u32[]{:S(2)}) copy-start(bf16[256,8192]{1,0:T(8,128)(2,1)} %own_ref.3) | copy-start | bytes 12582916
  66.8 7.7 %collective-permute-start.13 = (bf16[512,256]{1,0:T(8,128)(2,1)S(1)}, bf16[512,256]{1,0:T(8,128)(2,1)S(1)}, u32[]{:S(2)}, u32[]{:S(2)}) collective-permute-start(bf16[512,256]{1,0:T(8,128)(2,1)S(1)} %get-tuple-element.39), channel_id=1, source_target_pairs={{0,8},{1,9},{2,10},{3,11},{4,12},{5,13},{6,14},{7,15},{16,80},{17,... | collective-permute-start | bytes 786440 | tf_op jit(solution)/shard_map/ppermute | solution.py:356
  68.0 9.2 %collective-permute-start.14 = (bf16[512,256]{1,0:T(8,128)(2,1)S(1)}, bf16[512,256]{1,0:T(8,128)(2,1)S(1)}, u32[]{:S(2)}, u32[]{:S(2)}) collective-permute-start(bf16[512,256]{1,0:T(8,128)(2,1)S(1)} %get-tuple-element.40), channel_id=1, source_target_pairs={{0,32},{1,33},{2,34},{3,35},{4,36},{5,37},{6,38},{7,39},{16,144},{... | collective-permute-start | bytes 786440 | tf_op jit(solution)/shard_map/ppermute | solution.py:356
  70.4 6.9 %collective-permute-start.15 = (bf16[512,256]{1,0:T(8,128)(2,1)S(1)}, bf16[512,256]{1,0:T(8,128)(2,1)S(1)}, u32[]{:S(2)}, u32[]{:S(2)}) collective-permute-start(bf16[512,256]{1,0:T(8,128)(2,1)S(1)} %get-tuple-element.41), channel_id=1, source_target_pairs={{0,40},{1,41},{2,42},{3,43},{4,44},{5,45},{6,46},{7,47},{16,208},{... | collective-permute-start | bytes 786440 | tf_op jit(solution)/shard_map/ppermute | solution.py:356
  71.6 6.5 %collective-permute-start.12 = (bf16[8,32,512]{2,1,0:T(8,128)(2,1)S(1)}, bf16[8,32,512]{2,1,0:T(8,128)(2,1)S(1)}, u32[]{:S(2)}, u32[]{:S(2)}) collective-permute-start(bf16[8,32,512]{2,1,0:T(8,128)(2,1)S(1)} %slice.7), channel_id=1, source_target_pairs={{0,7},{1,0},{2,1},{3,2},{4,3},{5,4},{6,5},{7,6},{8,15},{9,8},{10,9... | collective-permute-start | bytes 786440 | tf_op jit(solution)/shard_map/ppermute | solution.py:322
  74.4 6.5 %collective-permute-start.11 = (bf16[8,32,512]{2,1,0:T(8,128)(2,1)S(1)}, bf16[8,32,512]{2,1,0:T(8,128)(2,1)S(1)}, u32[]{:S(2)}, u32[]{:S(2)}) collective-permute-start(bf16[8,32,512]{2,1,0:T(8,128)(2,1)S(1)} %slice.6), channel_id=1, source_target_pairs={{0,1},{1,2},{2,3},{3,4},{4,5},{5,6},{6,7},{7,0},{8,9},{9,10},{10,1... | collective-permute-start | bytes 786440 | tf_op jit(solution)/shard_map/ppermute | solution.py:322
  80.9 19.4 %copy-start.3 = (bf16[32,256,256]{2,1,0:T(8,128)(2,1)S(1)}, bf16[32,256,256]{2,1,0:T(8,128)(2,1)}, u32[]{:S(2)}) copy-start(bf16[32,256,256]{2,1,0:T(8,128)(2,1)} %copy-done.2) | copy-start | bytes 12582916
  85.4 14.9 %collective-permute-start.16 = (f32[256,512]{1,0:T(8,128)S(1)}, f32[256,512]{1,0:T(8,128)S(1)}, u32[]{:S(2)}, u32[]{:S(2)}) collective-permute-start(f32[256,512]{1,0:T(8,128)S(1)} %get-tuple-element.45), channel_id=1, source_target_pairs={{0,16},{16,0},{1,17},{17,1},{2,18},{18,2},{3,19},{19,3},{4,20},{20... | collective-permute-start | bytes 1572872 | tf_op jit(solution)/shard_map/ppermute | solution.py:18
  89.9 5.1 %collective-permute-start.17 = (bf16[4,32,512]{2,1,0:T(8,128)(2,1)S(1)}, bf16[4,32,512]{2,1,0:T(8,128)(2,1)S(1)}, u32[]{:S(2)}, u32[]{:S(2)}) collective-permute-start(bf16[4,32,512]{2,1,0:T(8,128)(2,1)S(1)} %get-tuple-element.42), channel_id=1, source_target_pairs={{0,1},{1,0},{2,3},{3,2},{4,5},{5,4},{6,7},{7,6},{8,9},{9,8},{10,11... | collective-permute-start | bytes 393224 | tf_op jit(solution)/shard_map/ppermute | solution.py:393
  95.5 8.1 %collective-permute-start.18 = (bf16[32,512]{1,0:T(8,128)(2,1)S(1)}, bf16[32,512]{1,0:T(8,128)(2,1)S(1)}, u32[]{:S(2)}, u32[]{:S(2)}) collective-permute-start(bf16[32,512]{1,0:T(8,128)(2,1)S(1)} %get-tuple-element.48), channel_id=1, source_target_pairs={{0,2},{1,3},{2,4},{3,5},{4,6},{5,7},{6,0},{7,1},{8,10},{9,11},{10,... | collective-permute-start | bytes 98312 | tf_op jit(solution)/shard_map/ppermute | solution.py:322
  95.6 8.0 %collective-permute-start.19 = (bf16[32,512]{1,0:T(8,128)(2,1)S(1)}, bf16[32,512]{1,0:T(8,128)(2,1)S(1)}, u32[]{:S(2)}, u32[]{:S(2)}) collective-permute-start(bf16[32,512]{1,0:T(8,128)(2,1)S(1)} %get-tuple-element.50), channel_id=1, source_target_pairs={{0,4},{1,5},{2,6},{3,7},{4,0},{5,1},{6,2},{7,3},{8,12},{9,13},{10,... | collective-permute-start | bytes 98312 | tf_op jit(solution)/shard_map/ppermute | solution.py:322
  97.2 6.4 %collective-permute-start.20 = (bf16[32,512]{1,0:T(8,128)(2,1)S(1)}, bf16[32,512]{1,0:T(8,128)(2,1)S(1)}, u32[]{:S(2)}, u32[]{:S(2)}) collective-permute-start(bf16[32,512]{1,0:T(8,128)(2,1)S(1)} %get-tuple-element.51), channel_id=1, source_target_pairs={{0,6},{1,7},{2,0},{3,1},{4,2},{5,3},{6,4},{7,5},{8,14},{9,15},{10,... | collective-permute-start | bytes 98312 | tf_op jit(solution)/shard_map/ppermute | solution.py:322
  (1 other events, 1.6 us)

commit v2 on v1

--- a/solution.py
+++ b/solution.py
@@ -22,53 +22,71 @@
     return pltpu.CompilerParams(vmem_limit_bytes=mib * MIB)
 
 
-def pick_kernel(place, act_ref, out_ref, sems):
-    blocks = out_ref.shape[1] // 512
-    copies = []
+INSIDE = pl.BlockSpec(memory_space=pltpu.VMEM)
+OUTSIDE = pl.BlockSpec(memory_space=pl.ANY)
+HBM = pl.BlockSpec(memory_space=pltpu.HBM)
+SCALARS = pl.BlockSpec(memory_space=pltpu.SMEM)
+
+
+def copies_of(pairs, sems):
+    return [pltpu.make_async_copy(a, b, sems.at[i]) for i, (a, b) in enumerate(pairs)]
+
+
+def start(copies):
+    for copy in copies:
+        copy.start()
+
+
+def columns(ref, i, width):
+    return ref.at[:, pl.ds(i * width, width)]
+
+
+def pick_kernel(place, act_hbm, out_hbm, held, si, so):
+    blocks = held.shape[0]
+    pairs = []
     for i in range(blocks):
         at = pl.multiple_of(i * 1024 + (1 - place[0]) * 512, 512)
-        copies.append(
-            pltpu.make_async_copy(
-                act_ref.at[:, pl.ds(at, 512)], out_ref.at[:, pl.ds(i * 512, 512)], sems.at[i]
-            )
-        )
-    for copy in copies:
-        copy.start()
-    for copy in copies:
+        pairs.append((act_hbm.at[:, pl.ds(at, 512)], held.at[i]))
+    incoming = copies_of(pairs, si)
+    outgoing = copies_of([(held.at[i], columns(out_hbm, i, 512)) for i in range(blocks)], so)
+    start(incoming)
+    for i in range(blocks):
+        incoming[i].wait()
+        outgoing[i].start()
+    for copy in outgoing:
         copy.wait()
 
 
 def other_half(place, activations):
     tokens, width = activations.shape
+    blocks = width // 1024
     return pl.pallas_call(
         pick_kernel,
         out_shape=jax.ShapeDtypeStruct((tokens, width // 2), BF),
-        in_specs=[pl.BlockSpec(memory_space=pltpu.SMEM), pl.BlockSpec(memory_space=pltpu.HBM)],
-        out_specs=pl.BlockSpec(memory_space=pltpu.VMEM),
-        scratch_shapes=[pltpu.SemaphoreType.DMA((width // 1024,))],
+        in_specs=[SCALARS, HBM],
+        out_specs=OUTSIDE,
+        scratch_shapes=[
+            pltpu.VMEM((blocks, tokens, 512), BF),
+            pltpu.SemaphoreType.DMA((blocks,)),
+            pltpu.SemaphoreType.DMA((blocks,)),
+        ],
         compiler_params=params(60),
         cost_estimate=pl.CostEstimate(flops=0, bytes_accessed=2 * tokens * width, transcendentals=0),
         name="other_half",
     )(place, activations)
 
 
-def copies_of(pairs, sems):
-    return [pltpu.make_async_copy(a, b, sems.at[i]) for i, (a, b) in enumerate(pairs)]
-
-
-def start(copies):
-    for copy in copies:
-        copy.start()
-
-
-def columns(ref, i, width):
-    return ref.at[:, pl.ds(i * width, width)]
-
-
-def weights_kernel(head_dim, q_ref, k_ref, cot_ref, segment_ref, p_ref, dv_ref):
-    length = q_ref.shape[0]
-    kv_heads = k_ref.shape[1] // head_dim
-    group = q_ref.shape[1] // k_ref.shape[1]
+def weights_kernel(
+    head_dim, q_hbm, k_ref, cot_hbm, segment_ref, p_hbm, dv_ref, q, cot, p, sq, sc, sp
+):
+    kv_heads, length, wide = q.shape
+    group = wide // head_dim
+    q_in = copies_of([(columns(q_hbm, g, wide), q.at[g]) for g in range(kv_heads)], sq)
+    cot_in = copies_of([(columns(cot_hbm, g, wide), cot.at[g]) for g in range(kv_heads)], sc)
+    pairs = [(p.at[g], p_hbm.at[pl.ds(g * group, group)]) for g in range(kv_heads)]
+    out = copies_of(pairs, sp)
+    for g in range(kv_heads):
+        start([q_in[g], cot_in[g]])
     row = segment_ref[...]
     column = jnp.broadcast_to(row.astype(F32), (128, length)).T[:, :1].astype(jnp.int32)
     u = lax.broadcasted_iota(jnp.int32, (length, length), 0)
@@ -76,27 +94,27 @@
     bias = jnp.where((u <= t) & (column == row), 0.0, -1e30)
     rate = math.log2(math.e) / math.sqrt(head_dim)
     for g in range(kv_heads):
+        if g < 2:
+            for copy in q_in[:1] + cot_in[:1] if g == 0 else q_in[1:] + cot_in[1:]:
+                copy.wait()
         total = jnp.zeros((length, head_dim), F32)
         own = slice(g * head_dim, (g + 1) * head_dim)
-        for h in range(g * group, (g + 1) * group):
+        for h in range(group):
             cols = slice(h * head_dim, (h + 1) * head_dim)
             scores = lax.dot_general(
-                k_ref[:, own], q_ref[:, cols], (((1,), (1,)), ((), ())), preferred_element_type=F32
+                k_ref[:, own], q[g, :, cols], (((1,), (1,)), ((), ())), preferred_element_type=F32
             )
             scores = scores + bias
             highest = jnp.max(scores, axis=0, keepdims=True)
             exponent = jnp.exp2((scores - highest) * rate)
             share = 1.0 / jnp.sum(exponent, axis=0, keepdims=True)
             probability = (exponent * share).astype(BF)
-            p_ref[h] = probability
-            total = total + jnp.dot(probability, cot_ref[:, cols], preferred_element_type=F32)
+            p[g, h] = probability
+            total = total + jnp.dot(probability, cot[g, :, cols], preferred_element_type=F32)
         dv_ref[:, own] = total.astype(BF)
-
-
-INSIDE = pl.BlockSpec(memory_space=pltpu.VMEM)
-OUTSIDE = pl.BlockSpec(memory_space=pl.ANY)
-HBM = pl.BlockSpec(memory_space=pltpu.HBM)
-SCALARS = pl.BlockSpec(memory_space=pltpu.SMEM)
+        out[g].start()
+    for copy in out:
+        copy.wait()
 
 
 def cost(flops, mib, exps=0):
@@ -113,19 +131,25 @@
             jax.ShapeDtypeStruct((heads, length, length), BF),
             jax.ShapeDtypeStruct(keys.shape, BF),
         ),
-        in_specs=[INSIDE] * 4,
-        out_specs=(INSIDE, INSIDE),
-        compiler_params=params(),
+        in_specs=[HBM, INSIDE, HBM, INSIDE],
+        out_specs=(HBM, INSIDE),
+        scratch_shapes=[
+            pltpu.VMEM((kv_heads, length, width // kv_heads), BF),
+            pltpu.VMEM((kv_heads, length, width // kv_heads), BF),
+            pltpu.VMEM((kv_heads, heads // kv_heads, length, length), BF),
+        ]
+        + [pltpu.SemaphoreType.DMA((kv_heads,))] * 3,
+        compiler_params=params(60),
         cost_estimate=cost(4 * width * length * length, 16, heads * length * length),
         name="attention_weights",
     )(queries, keys, cotangent, segment_ids)
 
 
-def product_kernel(factor, place, own_ref, got_ref, dvo_ref, dvg_ref, *outs):
+def product_kernel(factor, chunks, place, own_ref, got_ref, dvo_ref, dvg_ref, *outs):
     c, y, x = place[0], place[2], place[3]
     dv_own = dvo_ref[...].astype(F32).T.astype(BF)
     dv_got = dvg_ref[...].astype(F32).T.astype(BF)
-    for k in (1, 2, 3, 0):
+    for out_ref, k in zip(outs, chunks):
         for m in range(4):
             ty = jnp.where(c == 0, (y + k) % 4, m)
             tx = jnp.where(c == 0, m, (x + k) % 4)
@@ -134,19 +158,19 @@
             rows = jnp.dot(
                 dv_own, own_ref[:, pl.ds(at_own, 256)], preferred_element_type=F32
             ) + jnp.dot(dv_got, got_ref[:, pl.ds(at_got, 256)], preferred_element_type=F32)
-            outs[k][m] = (rows * factor).astype(BF)
-
-
-def product(place, act_own, act_got, dv_own, dv_got, factor):
+            out_ref[m] = (rows * factor).astype(BF)
+
+
+def product(place, act_own, act_got, dv_own, dv_got, factor, chunks):
     tokens, width = act_own.shape
     wide = dv_own.shape[1]
     return pl.pallas_call(
-        functools.partial(product_kernel, factor),
-        out_shape=(jax.ShapeDtypeStruct((4, wide, 256), BF),) * 4,
+        functools.partial(product_kernel, factor, chunks),
+        out_shape=(jax.ShapeDtypeStruct((4, wide, 256), BF),) * len(chunks),
         in_specs=[SCALARS] + [INSIDE] * 4,
-        out_specs=(INSIDE,) * 4,
-        compiler_params=params(),
-        cost_estimate=cost(2 * tokens * width * wide, 12),
+        out_specs=(INSIDE,) * len(chunks),
+        compiler_params=params(),
+        cost_estimate=cost(tokens * width * wide * len(chunks) // 2, 3 * len(chunks)),
         name="product",
     )(place, act_own, act_got, dv_own, dv_got)
 
@@ -322,25 +346,12 @@
     return lax.ppermute(array, "z", [(z, (z + k) % NZ) for z in range(NZ)])
 
 
-def gather_near(weight):
-    rows, wide = weight.shape
-    places = NY * NX
-    return exchange(jnp.tile(weight, (places, 1)), PLANE).reshape(places, rows, wide)
-
-
-def gather_first(near):
-    return along_z(near, 1), along_z(near, -1)
-
-
-def gather_rest(near, up, down, product_part, far_sum):
-    pieces = [near, up, down]
-    up, down = after(up, product_part), after(down, product_part)
-    for _ in range(2):
-        up, down = along_z(up, 1), along_z(down, -1)
-        pieces += [up, down]
-    half = near.shape[0] // 2
-    up, down = after(up, far_sum), after(down, far_sum)
-    return pieces + [along_z(up[:half], 1), along_z(down[half:], -1)]
+def gather_near(tiles, shape):
+    return exchange(tiles, PLANE).reshape((NY * NX,) + shape)
+
+
+def ring_step(up, down, other):
+    return along_z(after(up, other), 1), along_z(after(down, other), -1)
 
 
 def along(array, k, far):
@@ -360,8 +371,7 @@
     return [parts[0]] + [along(parts[k], k, far) for k in (1, 2, 3)]
 
 
-def reduce_last(place, keep, got, attended):
-    parts = add_pair(place, keep, got)
+def reduce_last(parts, attended):
     moved = [along_z(parts[j], 2 * j) for j in (1, 2, 3)]
     total = parts[0] + after(moved[0], attended).astype(F32)
     return total + moved[1].astype(F32) + moved[2].astype(F32)
@@ -380,21 +390,28 @@
         value_codes.astype(F32).reshape(rows_here, kv_heads, -1) * value_scales[:, :, None]
     ).reshape(rows_here, -1).astype(BF)
     factor = 1.0 / math.sqrt(activations.shape[0] * NY * NX * NC * NZ)
+    tiles = jnp.tile(weight, (NY * NX, 1))
     act_got = swap_cores(other_half(place, activations))
-    near = gather_near(weight)
+    near = gather_near(tiles, weight.shape)
     probability, dvalue = attention_weights(queries, keys, segment_ids, cotangent, kv_heads)
     dv_got = swap_cores(dvalue)
     near = after(near, dv_got)
-    up, down = gather_first(near)
-    parts = product(place, activations, act_got, dvalue, dv_got, factor)
-    far_sums = add_far(place, spread(parts, True))
-    pieces = gather_rest(near, up, down, parts[0], far_sums[0])
+    first = ring_step(near, near, dv_got)
+    sides = (place, activations, act_got, dvalue, dv_got, factor)
+    away = product(*sides, (1, 2, 3))
+    (here,) = product(*sides, (0,))
+    second = ring_step(*first, away[0])
+    far_sums = add_far(place, [here] + [along(away[k - 1], k, True) for k in (1, 2, 3)])
     keep, send = add_near(place, spread(far_sums, False))
     got = lax.ppermute(send, "z", [(z, z ^ 1) for z in range(NZ)])
-    pieces[-1] = after(pieces[-1], send)
+    sums = add_pair(place, keep, got)
+    third = ring_step(*second, near)
+    half = near.shape[0] // 2
+    last = ring_step(third[0][:half], third[1][half:], far_sums[0])
+    pieces = [near, *first, *second, *third, last[0], after(last[1], sums[1])]
     values_own, values_other = partial_values(place, activations, act_got, pieces)
     attended = attend(probability, values_own, swap_cores(values_other), kv_heads)
-    return (attended, reduce_last(place, keep, got, attended))
+    return (attended, reduce_last(sums, attended))
 
 
 def solution(mesh):

time: 105 us -> 98.4 us (0.937)
  waiting for transfers between devices: 30.8 us -> 24.1 us
  local copies, waits for them, and re-layouts: 6.84 us -> 4.23 us
  Pallas kernels: 22.9 us -> 24.7 us
  starting transfers between devices: 41.5 us -> 42.9 us
    pallas_call x1, Pallas kernels: 5.05 us -> 8.83 us  [attention_weights(): pl.pallas_call(functools.partial(weights_kernel, head_dim), out_shape=(ja...]
    ppermute x11, waiting for transfers between devices: 11.7 us -> 8.91 us  [along_z(): return lax.ppermute(array, 'z', [(z, (z + k) % NZ) for z in range(NZ)])]
    ppermute x6, waiting for transfers between devices: 11.9 us -> 9.19 us  [along(): return lax.ppermute(array, AXES, pairs)]
    unnamed x23 -> x15, local copies, waits for them, and re-layouts: 5.86 us -> 3.24 us
    ppermute x11, starting transfers between devices: 19.9 us -> 21.9 us  [along_z(): return lax.ppermute(array, 'z', [(z, (z + k) % NZ) for z in range(NZ)])]
    pallas_call x1, Pallas kernels: 4.49 us -> 3.29 us  [partial_values(): pl.pallas_call(values_kernel, out_shape=(jax.ShapeDtypeStruct((tokens, wi...]
    pallas_call x1 -> x2, Pallas kernels: 4 us -> 3.71 us  [product(): pl.pallas_call(functools.partial(product_kernel, factor, chunks), out_sha...]
  transfers between devices with their start and end apart: 22 -> 22, of which waited for: 8 -> 6; matrix products, arithmetic and copies ran while one was open for 1% -> 1% of each run, Pallas kernels for 14% -> 19%
where the time goes in v2:
time: 98.4 us; the launch traced here: 98.1 us
  starting transfers between devices  42.9 us (44%)
  Pallas kernels  24.7 us (25%)
  waiting for transfers between devices  24.1 us (24%)
  local copies, waits for them, and re-layouts  4.23 us (4%)
  other arithmetic  1.32 us (1%)
    ppermute x11, starting transfers between devices, along_z(): return lax.ppermute(array, 'z', [(z, (z + k) % NZ) for z in range(NZ)])  21.9 us
    ppermute x6, waiting for transfers between devices, along(): return lax.ppermute(array, AXES, pairs)  9.19 us
    ppermute x11, waiting for transfers between devices, along_z(): return lax.ppermute(array, 'z', [(z, (z + k) % NZ) for z in range(NZ)])  8.91 us
    pallas_call x1, Pallas kernels, attention_weights(): pl.pallas_call(functools.partial(weights_kernel, head_dim), out_shape=(ja...  8.83 us
    ppermute x6, starting transfers between devices, along(): return lax.ppermute(array, AXES, pairs)  8.77 us
    ppermute x3, starting transfers between devices, swap_cores(): return lax.ppermute(array, 'c', [(0, 1), (1, 0)])  7.08 us
    all_to_all x1, starting transfers between devices, exchange(): return lax.all_to_all(array, axes, 0, 0, tiled=True)  5.02 us
    ppermute x1, waiting for transfers between devices, local(): got = lax.ppermute(send, 'z', [(z, z ^ 1) for z in range(NZ)])  4.1 us
  transfers between devices with their start and end apart: 22, of which 6 were waited for; matrix products, arithmetic and copies ran while one was open for 1% of the time, Pallas kernels for 19%

profile of v2, /device:TPU:1, one launch (start us, length us, event | category | flops | bytes accessed | tf_op | source)
XLA Modules:
  0.0 98.1 jit_solution(15840779169930734452)
XLA Ops:
  0.6 0.7 pad_add_fusion.place
  1.3 3.2 %other_half.1 = bf16[256,4096]{1,0:T(8,128)(2,1)} custom-call(s32[4]{0:T(128)} %pad_add_fusion.place, bf16[256,8192]{1,0:T(8,128)(2,1)} %own_ref.5), custom_call_target="tpu_custom_call" | custom-call | bytes 4194304 | tf_op jit(solution)/shard_map/other_half/pallas_call | solution.py:63
  4.5 3.3 %collective-permute-start = (bf16[256,4096]{1,0:T(8,128)(2,1)}, bf16[256,4096]{1,0:T(8,128)(2,1)S(1)}, u32[]{:S(2)}, u32[]{:S(2)}) collective-permute-start(bf16[256,4096]{1,0:T(8,128)(2,1)} %other_half.1), channel_id=1, source_target_pairs={{0,16},{16,0},{1,17},{17,1},{2,18},{18,2},{3,19},{19,3},{4,20},{20... | collective-permute-start | bytes 6291464 | tf_op jit(solution)/shard_map/ppermute | solution.py:18
  8.0 0.9 tile.2
  8.9 5.0 %all-to-all-start = ((bf16[16,32,512]{2,1,0:T(8,128)(2,1)}), bf16[16,32,512]{2,1,0:T(8,128)(2,1)S(1)}, u32[]{:S(2)}, u32[]{:S(2)}) async-start(bf16[16,32,512]{2,1,0:T(8,128)(2,1)} %tile.2), calls=%async_computation | async-start | bytes 1048576 | tf_op jit(solution)/shard_map/all_to_all | solution.py:342
  14.0 8.8 %attention_weights.1 = (bf16[32,256,256]{2,1,0:T(8,128)(2,1)}, bf16[256,512]{1,0:T(8,128)(2,1)}) custom-call(bf16[256,4096]{1,0:T(8,128)(2,1)} %q_hbm.1, bf16[256,512]{1,0:T(8,128)(2,1)} %k_ref.1, bf16[256,4096]{1,0:T(8,128)(2,1)} %cot_hbm.1, s32[1,256]{1,0:T(1,128)} %segment_ref.1), custom_call_target="tpu_custom_call" | custom-call | flops 1073741824 | bytes 16777216 | tf_op jit(solution)/shard_map/attention_weights/pallas_call | solution.py:128
  23.2 1.5 %collective-permute-done.1.dvg_ref = bf16[256,512]{1,0:T(8,128)(2,1)S(1)} collective-permute-done((bf16[256,512]{1,0:T(8,128)(2,1)}, bf16[256,512]{1,0:T(8,128)(2,1)S(1)}, u32[]{:S(2)}, u32[]{:S(2)}) %collective-permute-start.1) | collective-permute-done | bytes 262176 | tf_op jit(solution)/shard_map/ppermute | solution.py:18
  25.0 5.6 %collective-permute-start.3 = (bf16[16,32,512]{2,1,0:T(8,128)(2,1)S(1)}, bf16[16,32,512]{2,1,0:T(8,128)(2,1)S(1)}, u32[]{:S(2)}, u32[]{:S(2)}) collective-permute-start(bf16[16,32,512]{2,1,0:T(8,128)(2,1)S(1)} %all-to-all-done.refs_0_), channel_id=1, source_target_pairs={{0,7},{1,0},{2,1},{3,2},{4,3},{5,4},{6,5},{7,6},{8,15},{9,8},{10,9... | collective-permute-start | bytes 1572872 | tf_op jit(solution)/shard_map/ppermute | solution.py:346
  30.6 2.2 %copy-done = bf16[256,8192]{1,0:T(8,128)(2,1)S(1)} copy-done((bf16[256,8192]{1,0:T(8,128)(2,1)S(1)}, bf16[256,8192]{1,0:T(8,128)(2,1)}, u32[]{:S(2)}) %copy-start) | copy-done | bytes 4194328
  32.8 0.9 copy-done.3
  33.8 2.4 %product.2 = (bf16[4,512,256]{2,1,0:T(8,128)(2,1)S(1)}, bf16[4,512,256]{2,1,0:T(8,128)(2,1)S(1)}, bf16[4,512,256]{2,1,0:T(8,128)(2,1)S(1)}) custom-call(s32[4]{0:T(128)S(1)} %copy-done.4, bf16[256,8192]{1,0:T(8,128)(2,1)S(1)} %copy-done, bf16[256,4096]{1,0:T(8,128)(2,1)S(1)} %collective-permute-done.got_ref, bf16[256,512]{1,0:T(8,128)(2,1)S(1)} %copy-done.3, ...), custom_call_target="tpu_custom_call" | custom-call | flops 1610612736 | bytes 9437184 | tf_op jit(solution)/shard_map/product/pallas_call | solution.py:167
  36.2 1.3 %collective-permute-start.8 = (bf16[4,512,256]{2,1,0:T(8,128)(2,1)S(1)}, bf16[4,512,256]{2,1,0:T(8,128)(2,1)S(1)}, u32[]{:S(2)}, u32[]{:S(2)}) collective-permute-start(bf16[4,512,256]{2,1,0:T(8,128)(2,1)S(1)} %get-tuple-element.33), channel_id=1, source_target_pairs={{0,64},{1,65},{2,66},{3,67},{4,68},{5,69},{6,70},{7,71},{16,24},{1... | collective-permute-start | bytes 3145736 | tf_op jit(solution)/shard_map/ppermute | solution.py:367
  37.4 1.5 %collective-permute-start.10 = (bf16[4,512,256]{2,1,0:T(8,128)(2,1)S(1)}, bf16[4,512,256]{2,1,0:T(8,128)(2,1)S(1)}, u32[]{:S(2)}, u32[]{:S(2)}) collective-permute-start(bf16[4,512,256]{2,1,0:T(8,128)(2,1)S(1)} %get-tuple-element.39), channel_id=1, source_target_pairs={{0,192},{1,193},{2,194},{3,195},{4,196},{5,197},{6,198},{7,199},{1... | collective-permute-start | bytes 3145736 | tf_op jit(solution)/shard_map/ppermute | solution.py:367
  38.9 1.5 %collective-permute-start.9 = (bf16[4,512,256]{2,1,0:T(8,128)(2,1)S(1)}, bf16[4,512,256]{2,1,0:T(8,128)(2,1)S(1)}, u32[]{:S(2)}, u32[]{:S(2)}) collective-permute-start(bf16[4,512,256]{2,1,0:T(8,128)(2,1)S(1)} %get-tuple-element.38), channel_id=1, source_target_pairs={{0,128},{1,129},{2,130},{3,131},{4,132},{5,133},{6,134},{7,135},{1... | collective-permute-start | bytes 3145736 | tf_op jit(solution)/shard_map/ppermute | solution.py:367
  40.4 3.4 %collective-permute-start.5 = (bf16[16,32,512]{2,1,0:T(8,128)(2,1)S(1)}, bf16[16,32,512]{2,1,0:T(8,128)(2,1)S(1)}, u32[]{:S(2)}, u32[]{:S(2)}) collective-permute-start(bf16[16,32,512]{2,1,0:T(8,128)(2,1)S(1)} %collective-permute-done.3.refs_2_), channel_id=1, source_target_pairs={{0,7},{1,0},{2,1},{3,2},{4,3},{5,4},{6,5},{7,6},{8,15},{9,8},{10,9... | collective-permute-start | bytes 1572872 | tf_op jit(solution)/shard_map/ppermute | solution.py:346
  43.8 8.9 %collective-permute-done.5.refs_4_ = bf16[16,32,512]{2,1,0:T(8,128)(2,1)S(1)} collective-permute-done((bf16[16,32,512]{2,1,0:T(8,128)(2,1)S(1)}, bf16[16,32,512]{2,1,0:T(8,128)(2,1)S(1)}, u32[]{:S(2)}, u32[]{:S(2)}) %collective-permute-start.5) | collective-permute-done | bytes 524320 | tf_op jit(solution)/shard_map/ppermute | solution.py:346
  52.7 3.4 %collective-permute-start.7 = (bf16[16,32,512]{2,1,0:T(8,128)(2,1)S(1)}, bf16[16,32,512]{2,1,0:T(8,128)(2,1)S(1)}, u32[]{:S(2)}, u32[]{:S(2)}) collective-permute-start(bf16[16,32,512]{2,1,0:T(8,128)(2,1)S(1)} %collective-permute-done.5.refs_4_), channel_id=1, source_target_pairs={{0,7},{1,0},{2,1},{3,2},{4,3},{5,4},{6,5},{7,6},{8,15},{9,8},{10,9... | collective-permute-start | bytes 1572872 | tf_op jit(solution)/shard_map/ppermute | solution.py:346
  56.1 1.3 %product.3.refs_0_ = bf16[4,512,256]{2,1,0:T(8,128)(2,1)S(1)} custom-call(s32[4]{0:T(128)S(1)} %copy-done.4, bf16[256,8192]{1,0:T(8,128)(2,1)S(1)} %copy-done, bf16[256,4096]{1,0:T(8,128)(2,1)S(1)} %collective-permute-done.got_ref, bf16[256,512]{1,0:T(8,128)(2,1)S(1)} %copy-done.3, bf16[256,512]{1,0:T(8,128)(2,1)S(1)} %collective-permute-done.1.dvg_ref), custom_call_target="tpu_custom_call" | custom-call | flops 536870912 | bytes 3145728 | tf_op jit(solution)/shard_map/product/pallas_call | solution.py:167
  57.4 6.1 %collective-permute-done.9.refs_2_ = bf16[4,512,256]{2,1,0:T(8,128)(2,1)S(1)} collective-permute-done((bf16[4,512,256]{2,1,0:T(8,128)(2,1)S(1)}, bf16[4,512,256]{2,1,0:T(8,128)(2,1)S(1)}, u32[]{:S(2)}, u32[]{:S(2)}) %collective-permute-start.9) | collective-permute-done | bytes 1048608 | tf_op jit(solution)/shard_map/ppermute | solution.py:367
  63.6 1.1 %add_far.1 = (bf16[512,256]{1,0:T(8,128)(2,1)S(1)}, bf16[512,256]{1,0:T(8,128)(2,1)S(1)}, bf16[512,256]{1,0:T(8,128)(2,1)S(1)}, bf16[512,256]{1,0:T(8,128)(2,1)S(1)}) custom-call(s32[4]{0:T(128)S(1)} %copy-done.4, bf16[4,512,256]{2,1,0:T(8,128)(2,1)S(1)} %product.3.refs_0_, bf16[4,512,256]{2,1,0:T(8,128)(2,1)S(1)} %collective-permute-done.8.refs_1_, ...), custom_call_target="tpu_custom_call" | custom-call | flops 2097152 | bytes 5242880 | tf_op jit(solution)/shard_map/add_far/pallas_call | solution.py:236
  64.6 1.0 collective-permute-start.13
  65.6 2.7 %collective-permute-start.14 = (bf16[512,256]{1,0:T(8,128)(2,1)S(1)}, bf16[512,256]{1,0:T(8,128)(2,1)S(1)}, u32[]{:S(2)}, u32[]{:S(2)}) collective-permute-start(bf16[512,256]{1,0:T(8,128)(2,1)S(1)} %get-tuple-element.44), channel_id=1, source_target_pairs={{0,32},{1,33},{2,34},{3,35},{4,36},{5,37},{6,38},{7,39},{16,144},{... | collective-permute-start | bytes 786440 | tf_op jit(solution)/shard_map/ppermute | solution.py:367
  68.3 0.9 collective-permute-start.15
  69.2 2.7 %collective-permute-start.12 = (bf16[8,32,512]{2,1,0:T(8,128)(2,1)S(1)}, bf16[8,32,512]{2,1,0:T(8,128)(2,1)S(1)}, u32[]{:S(2)}, u32[]{:S(2)}) collective-permute-start(bf16[8,32,512]{2,1,0:T(8,128)(2,1)S(1)} %slice.9), channel_id=1, source_target_pairs={{0,7},{1,0},{2,1},{3,2},{4,3},{5,4},{6,5},{7,6},{8,15},{9,8},{10,9... | collective-permute-start | bytes 786440 | tf_op jit(solution)/shard_map/ppermute | solution.py:346
  72.1 3.1 %collective-permute-done.14.refs_2_ = bf16[512,256]{1,0:T(8,128)(2,1)S(1)} collective-permute-done((bf16[512,256]{1,0:T(8,128)(2,1)S(1)}, bf16[512,256]{1,0:T(8,128)(2,1)S(1)}, u32[]{:S(2)}, u32[]{:S(2)}) %collective-permute-start.14) | collective-permute-done | bytes 262176 | tf_op jit(solution)/shard_map/ppermute | solution.py:367
  75.1 0.8 add_near.1
  76.1 4.1 %collective-permute-done.16.got_ref = bf16[4,32,512]{2,1,0:T(8,128)(2,1)S(1)} collective-permute-done((bf16[4,32,512]{2,1,0:T(8,128)(2,1)S(1)}, bf16[4,32,512]{2,1,0:T(8,128)(2,1)S(1)}, u32[]{:S(2)}, u32[]{:S(2)}) %collective-permute-start.16) | collective-permute-done | bytes 131104 | tf_op jit(solution)/shard_map/ppermute | solution.py:406
  80.8 3.3 %partial_values.1 = (f32[256,512]{1,0:T(8,128)S(1)}, f32[256,512]{1,0:T(8,128)S(1)}) custom-call(s32[4]{0:T(128)S(1)} %copy-done.4, bf16[256,8192]{1,0:T(8,128)(2,1)S(1)} %copy-done.1, bf16[256,4096]{1,0:T(8,128)(2,1)S(1)} %collective-permute-done.got_ref, bf16[16,32,512]{2,1,0:T(8,128)(2,1)S(1)} %all-to-all-done.refs_0_, ...), custom_call_target="tpu_custom_call" | custom-call | flops 2147483648 | bytes 12582912 | tf_op jit(solution)/shard_map/partial_values/pallas_call | solution.py:208
  84.1 3.4 %collective-permute-start.17 = (f32[256,512]{1,0:T(8,128)S(1)}, f32[256,512]{1,0:T(8,128)S(1)}, u32[]{:S(2)}, u32[]{:S(2)}) collective-permute-start(f32[256,512]{1,0:T(8,128)S(1)} %get-tuple-element.51), channel_id=1, source_target_pairs={{0,16},{16,0},{1,17},{17,1},{2,18},{18,2},{3,19},{19,3},{4,20},{20... | collective-permute-start | bytes 1572872 | tf_op jit(solution)/shard_map/ppermute | solution.py:18
  87.7 4.2 %collective-permute-start.19 = (bf16[32,512]{1,0:T(8,128)(2,1)S(1)}, bf16[32,512]{1,0:T(8,128)(2,1)S(1)}, u32[]{:S(2)}, u32[]{:S(2)}) collective-permute-start(bf16[32,512]{1,0:T(8,128)(2,1)S(1)} %get-tuple-element.54), channel_id=1, source_target_pairs={{0,4},{1,5},{2,6},{3,7},{4,0},{5,1},{6,2},{7,3},{8,12},{9,13},{10,... | collective-permute-start | bytes 98312 | tf_op jit(solution)/shard_map/ppermute | solution.py:346
  92.0 2.2 %collective-permute-start.20 = (bf16[32,512]{1,0:T(8,128)(2,1)S(1)}, bf16[32,512]{1,0:T(8,128)(2,1)S(1)}, u32[]{:S(2)}, u32[]{:S(2)}) collective-permute-start(bf16[32,512]{1,0:T(8,128)(2,1)S(1)} %get-tuple-element.55), channel_id=1, source_target_pairs={{0,6},{1,7},{2,0},{3,1},{4,2},{5,3},{6,4},{7,5},{8,14},{9,15},{10,... | collective-permute-start | bytes 98312 | tf_op jit(solution)/shard_map/ppermute | solution.py:346
  94.1 3.2 %attend.1 = bf16[256,4096]{1,0:T(8,128)(2,1)} custom-call(bf16[32,256,256]{2,1,0:T(8,128)(2,1)S(1)} %copy-done.2, f32[256,512]{1,0:T(8,128)S(1)} %get-tuple-element.50.vo_ref, f32[256,512]{1,0:T(8,128)S(1)} %collective-permute-done.17.vg_ref), custom_call_target="tpu_custom_call" | custom-call | flops 536870912 | bytes 8388608 | tf_op jit(solution)/shard_map/attend/pallas_call | solution.py:321
  (43 shorter events, 2.7 us)
Async XLA Ops:
  1.3 6.5 %copy-start.6 = (f32[32,4]{0,1:T(4,128)S(1)}, f32[32,4]{0,1:T(4,128)}, u32[]{:S(2)}) copy-start(f32[32,4]{0,1:T(4,128)} %param.13) | copy-start | bytes 1540
  1.3 6.7 %copy-start.5 = (bf16[32,512]{1,0:T(8,128)(2,1)S(1)}, bf16[32,512]{1,0:T(8,128)(2,1)}, u32[]{:S(2)}) copy-start(bf16[32,512]{1,0:T(8,128)(2,1)} %param.12) | copy-start | bytes 98308
  4.5 26.1 %collective-permute-start = (bf16[256,4096]{1,0:T(8,128)(2,1)}, bf16[256,4096]{1,0:T(8,128)(2,1)S(1)}, u32[]{:S(2)}, u32[]{:S(2)}) collective-permute-start(bf16[256,4096]{1,0:T(8,128)(2,1)} %other_half.1), channel_id=1, source_target_pairs={{0,16},{16,0},{1,17},{17,1},{2,18},{18,2},{3,19},{19,3},{4,20},{20... | collective-permute-start | bytes 6291464 | tf_op jit(solution)/shard_map/ppermute | solution.py:18
  8.9 16.1 %all-to-all-start = ((bf16[16,32,512]{2,1,0:T(8,128)(2,1)}), bf16[16,32,512]{2,1,0:T(8,128)(2,1)S(1)}, u32[]{:S(2)}, u32[]{:S(2)}) async-start(bf16[16,32,512]{2,1,0:T(8,128)(2,1)} %tile.2), calls=%async_computation | async-start | bytes 1048576 | tf_op jit(solution)/shard_map/all_to_all | solution.py:342
  13.9 16.7 %copy-start.4 = (s32[4]{0:T(128)S(1)}, s32[4]{0:T(128)}, u32[]{:S(2)}) copy-start(s32[4]{0:T(128)} %pad_add_fusion.place) | copy-start | bytes 52
  22.8 1.8 %collective-permute-start.1 = (bf16[256,512]{1,0:T(8,128)(2,1)}, bf16[256,512]{1,0:T(8,128)(2,1)S(1)}, u32[]{:S(2)}, u32[]{:S(2)}) collective-permute-start(bf16[256,512]{1,0:T(8,128)(2,1)} %get-tuple-element.30.dvo_ref), channel_id=1, source_target_pairs={{0,16},{16,0},{1,17},{17,1},{2,18},{18,2},{3,19},{19,3},{4,20},{20... | collective-permute-start | bytes 786440 | tf_op jit(solution)/shard_map/ppermute | solution.py:18
  25.0 15.4 %collective-permute-start.3 = (bf16[16,32,512]{2,1,0:T(8,128)(2,1)S(1)}, bf16[16,32,512]{2,1,0:T(8,128)(2,1)S(1)}, u32[]{:S(2)}, u32[]{:S(2)}) collective-permute-start(bf16[16,32,512]{2,1,0:T(8,128)(2,1)S(1)} %all-to-all-done.refs_0_), channel_id=1, source_target_pairs={{0,7},{1,0},{2,1},{3,2},{4,3},{5,4},{6,5},{7,6},{8,15},{9,8},{10,9... | collective-permute-start | bytes 1572872 | tf_op jit(solution)/shard_map/ppermute | solution.py:346
  30.6 13.2 %collective-permute-start.2 = (bf16[16,32,512]{2,1,0:T(8,128)(2,1)S(1)}, bf16[16,32,512]{2,1,0:T(8,128)(2,1)S(1)}, u32[]{:S(2)}, u32[]{:S(2)}) collective-permute-start(bf16[16,32,512]{2,1,0:T(8,128)(2,1)S(1)} %all-to-all-done.refs_0_), channel_id=1, source_target_pairs={{0,1},{1,2},{2,3},{3,4},{4,5},{5,6},{6,7},{7,0},{8,9},{9,10},{10,1... | collective-permute-start | bytes 1572872 | tf_op jit(solution)/shard_map/ppermute | solution.py:346
  30.6 2.2 %copy-start = (bf16[256,8192]{1,0:T(8,128)(2,1)S(1)}, bf16[256,8192]{1,0:T(8,128)(2,1)}, u32[]{:S(2)}) copy-start(bf16[256,8192]{1,0:T(8,128)(2,1)} %own_ref.5) | copy-start | bytes 12582916
  32.8 0.9 copy-start.3
  36.2 21.3 %collective-permute-start.8 = (bf16[4,512,256]{2,1,0:T(8,128)(2,1)S(1)}, bf16[4,512,256]{2,1,0:T(8,128)(2,1)S(1)}, u32[]{:S(2)}, u32[]{:S(2)}) collective-permute-start(bf16[4,512,256]{2,1,0:T(8,128)(2,1)S(1)} %get-tuple-element.33), channel_id=1, source_target_pairs={{0,64},{1,65},{2,66},{3,67},{4,68},{5,69},{6,70},{7,71},{16,24},{1... | collective-permute-start | bytes 3145736 | tf_op jit(solution)/shard_map/ppermute | solution.py:367
  37.4 20.0 %collective-permute-start.10 = (bf16[4,512,256]{2,1,0:T(8,128)(2,1)S(1)}, bf16[4,512,256]{2,1,0:T(8,128)(2,1)S(1)}, u32[]{:S(2)}, u32[]{:S(2)}) collective-permute-start(bf16[4,512,256]{2,1,0:T(8,128)(2,1)S(1)} %get-tuple-element.39), channel_id=1, source_target_pairs={{0,192},{1,193},{2,194},{3,195},{4,196},{5,197},{6,198},{7,199},{1... | collective-permute-start | bytes 3145736 | tf_op jit(solution)/shard_map/ppermute | solution.py:367
  38.9 24.6 %collective-permute-start.9 = (bf16[4,512,256]{2,1,0:T(8,128)(2,1)S(1)}, bf16[4,512,256]{2,1,0:T(8,128)(2,1)S(1)}, u32[]{:S(2)}, u32[]{:S(2)}) collective-permute-start(bf16[4,512,256]{2,1,0:T(8,128)(2,1)S(1)} %get-tuple-element.38), channel_id=1, source_target_pairs={{0,128},{1,129},{2,130},{3,131},{4,132},{5,133},{6,134},{7,135},{1... | collective-permute-start | bytes 3145736 | tf_op jit(solution)/shard_map/ppermute | solution.py:367
  40.4 12.3 %collective-permute-start.5 = (bf16[16,32,512]{2,1,0:T(8,128)(2,1)S(1)}, bf16[16,32,512]{2,1,0:T(8,128)(2,1)S(1)}, u32[]{:S(2)}, u32[]{:S(2)}) collective-permute-start(bf16[16,32,512]{2,1,0:T(8,128)(2,1)S(1)} %collective-permute-done.3.refs_2_), channel_id=1, source_target_pairs={{0,7},{1,0},{2,1},{3,2},{4,3},{5,4},{6,5},{7,6},{8,15},{9,8},{10,9... | collective-permute-start | bytes 1572872 | tf_op jit(solution)/shard_map/ppermute | solution.py:346
  43.8 12.3 %collective-permute-start.4 = (bf16[16,32,512]{2,1,0:T(8,128)(2,1)S(1)}, bf16[16,32,512]{2,1,0:T(8,128)(2,1)S(1)}, u32[]{:S(2)}, u32[]{:S(2)}) collective-permute-start(bf16[16,32,512]{2,1,0:T(8,128)(2,1)S(1)} %collective-permute-done.2.refs_1_), channel_id=1, source_target_pairs={{0,1},{1,2},{2,3},{3,4},{4,5},{5,6},{6,7},{7,0},{8,9},{9,10},{10,1... | collective-permute-start | bytes 1572872 | tf_op jit(solution)/shard_map/ppermute | solution.py:346
  52.7 16.5 %collective-permute-start.7 = (bf16[16,32,512]{2,1,0:T(8,128)(2,1)S(1)}, bf16[16,32,512]{2,1,0:T(8,128)(2,1)S(1)}, u32[]{:S(2)}, u32[]{:S(2)}) collective-permute-start(bf16[16,32,512]{2,1,0:T(8,128)(2,1)S(1)} %collective-permute-done.5.refs_4_), channel_id=1, source_target_pairs={{0,7},{1,0},{2,1},{3,2},{4,3},{5,4},{6,5},{7,6},{8,15},{9,8},{10,9... | collective-permute-start | bytes 1572872 | tf_op jit(solution)/shard_map/ppermute | solution.py:346
  56.1 15.8 %collective-permute-start.6 = (bf16[16,32,512]{2,1,0:T(8,128)(2,1)S(1)}, bf16[16,32,512]{2,1,0:T(8,128)(2,1)S(1)}, u32[]{:S(2)}, u32[]{:S(2)}) collective-permute-start(bf16[16,32,512]{2,1,0:T(8,128)(2,1)S(1)} %collective-permute-done.4.refs_3_), channel_id=1, source_target_pairs={{0,1},{1,2},{2,3},{3,4},{4,5},{5,6},{6,7},{7,0},{8,9},{9,10},{10,1... | collective-permute-start | bytes 1572872 | tf_op jit(solution)/shard_map/ppermute | solution.py:346
  63.5 17.2 %copy-start.1 = (bf16[256,8192]{1,0:T(8,128)(2,1)S(1)}, bf16[256,8192]{1,0:T(8,128)(2,1)}, u32[]{:S(2)}) copy-start(bf16[256,8192]{1,0:T(8,128)(2,1)} %own_ref.5) | copy-start | bytes 12582916
  64.6 7.4 %collective-permute-start.13 = (bf16[512,256]{1,0:T(8,128)(2,1)S(1)}, bf16[512,256]{1,0:T(8,128)(2,1)S(1)}, u32[]{:S(2)}, u32[]{:S(2)}) collective-permute-start(bf16[512,256]{1,0:T(8,128)(2,1)S(1)} %get-tuple-element.43), channel_id=1, source_target_pairs={{0,8},{1,9},{2,10},{3,11},{4,12},{5,13},{6,14},{7,15},{16,80},{17,... | collective-permute-start | bytes 786440 | tf_op jit(solution)/shard_map/ppermute | solution.py:367
  65.6 9.6 %collective-permute-start.14 = (bf16[512,256]{1,0:T(8,128)(2,1)S(1)}, bf16[512,256]{1,0:T(8,128)(2,1)S(1)}, u32[]{:S(2)}, u32[]{:S(2)}) collective-permute-start(bf16[512,256]{1,0:T(8,128)(2,1)S(1)} %get-tuple-element.44), channel_id=1, source_target_pairs={{0,32},{1,33},{2,34},{3,35},{4,36},{5,37},{6,38},{7,39},{16,144},{... | collective-permute-start | bytes 786440 | tf_op jit(solution)/shard_map/ppermute | solution.py:367
  68.3 6.9 %collective-permute-start.15 = (bf16[512,256]{1,0:T(8,128)(2,1)S(1)}, bf16[512,256]{1,0:T(8,128)(2,1)S(1)}, u32[]{:S(2)}, u32[]{:S(2)}) collective-permute-start(bf16[512,256]{1,0:T(8,128)(2,1)S(1)} %get-tuple-element.45), channel_id=1, source_target_pairs={{0,40},{1,41},{2,42},{3,43},{4,44},{5,45},{6,46},{7,47},{16,208},{... | collective-permute-start | bytes 786440 | tf_op jit(solution)/shard_map/ppermute | solution.py:367
  69.2 11.6 %collective-permute-start.12 = (bf16[8,32,512]{2,1,0:T(8,128)(2,1)S(1)}, bf16[8,32,512]{2,1,0:T(8,128)(2,1)S(1)}, u32[]{:S(2)}, u32[]{:S(2)}) collective-permute-start(bf16[8,32,512]{2,1,0:T(8,128)(2,1)S(1)} %slice.9), channel_id=1, source_target_pairs={{0,7},{1,0},{2,1},{3,2},{4,3},{5,4},{6,5},{7,6},{8,15},{9,8},{10,9... | collective-permute-start | bytes 786440 | tf_op jit(solution)/shard_map/ppermute | solution.py:346
  72.0 8.8 %collective-permute-start.11 = (bf16[8,32,512]{2,1,0:T(8,128)(2,1)S(1)}, bf16[8,32,512]{2,1,0:T(8,128)(2,1)S(1)}, u32[]{:S(2)}, u32[]{:S(2)}) collective-permute-start(bf16[8,32,512]{2,1,0:T(8,128)(2,1)S(1)} %slice.8), channel_id=1, source_target_pairs={{0,1},{1,2},{2,3},{3,4},{4,5},{5,6},{6,7},{7,0},{8,9},{9,10},{10,1... | collective-permute-start | bytes 786440 | tf_op jit(solution)/shard_map/ppermute | solution.py:346
  76.0 4.2 %collective-permute-start.16 = (bf16[4,32,512]{2,1,0:T(8,128)(2,1)S(1)}, bf16[4,32,512]{2,1,0:T(8,128)(2,1)S(1)}, u32[]{:S(2)}, u32[]{:S(2)}) collective-permute-start(bf16[4,32,512]{2,1,0:T(8,128)(2,1)S(1)} %get-tuple-element.47), channel_id=1, source_target_pairs={{0,1},{1,0},{2,3},{3,2},{4,5},{5,4},{6,7},{7,6},{8,9},{9,8},{10,11... | collective-permute-start | bytes 393224 | tf_op jit(solution)/shard_map/ppermute | solution.py:406
  80.8 13.4 %copy-start.2 = (bf16[32,256,256]{2,1,0:T(8,128)(2,1)S(1)}, bf16[32,256,256]{2,1,0:T(8,128)(2,1)}, u32[]{:S(2)}) copy-start(bf16[32,256,256]{2,1,0:T(8,128)(2,1)} %get-tuple-element.29.p_hbm) | copy-start | bytes 12582916
  84.1 10.1 %collective-permute-start.17 = (f32[256,512]{1,0:T(8,128)S(1)}, f32[256,512]{1,0:T(8,128)S(1)}, u32[]{:S(2)}, u32[]{:S(2)}) collective-permute-start(f32[256,512]{1,0:T(8,128)S(1)} %get-tuple-element.51), channel_id=1, source_target_pairs={{0,16},{16,0},{1,17},{17,1},{2,18},{18,2},{3,19},{19,3},{4,20},{20... | collective-permute-start | bytes 1572872 | tf_op jit(solution)/shard_map/ppermute | solution.py:18
  87.5 9.9 %collective-permute-start.18 = (bf16[32,512]{1,0:T(8,128)(2,1)S(1)}, bf16[32,512]{1,0:T(8,128)(2,1)S(1)}, u32[]{:S(2)}, u32[]{:S(2)}) collective-permute-start(bf16[32,512]{1,0:T(8,128)(2,1)S(1)} %get-tuple-element.48), channel_id=1, source_target_pairs={{0,2},{1,3},{2,4},{3,5},{4,6},{5,7},{6,0},{7,1},{8,10},{9,11},{10,... | collective-permute-start | bytes 98312 | tf_op jit(solution)/shard_map/ppermute | solution.py:346
  87.7 9.7 %collective-permute-start.19 = (bf16[32,512]{1,0:T(8,128)(2,1)S(1)}, bf16[32,512]{1,0:T(8,128)(2,1)S(1)}, u32[]{:S(2)}, u32[]{:S(2)}) collective-permute-start(bf16[32,512]{1,0:T(8,128)(2,1)S(1)} %get-tuple-element.54), channel_id=1, source_target_pairs={{0,4},{1,5},{2,6},{3,7},{4,0},{5,1},{6,2},{7,3},{8,12},{9,13},{10,... | collective-permute-start | bytes 98312 | tf_op jit(solution)/shard_map/ppermute | solution.py:346
  92.0 5.5 %collective-permute-start.20 = (bf16[32,512]{1,0:T(8,128)(2,1)S(1)}, bf16[32,512]{1,0:T(8,128)(2,1)S(1)}, u32[]{:S(2)}, u32[]{:S(2)}) collective-permute-start(bf16[32,512]{1,0:T(8,128)(2,1)S(1)} %get-tuple-element.55), channel_id=1, source_target_pairs={{0,6},{1,7},{2,0},{3,1},{4,2},{5,3},{6,4},{7,5},{8,14},{9,15},{10,... | collective-permute-start | bytes 98312 | tf_op jit(solution)/shard_map/ppermute | solution.py:346

commit v3 on v2

--- a/solution.py
+++ b/solution.py
@@ -180,11 +180,14 @@
     rows, wide = pieces[0].shape[1:]
     c = place[0]
     places = weight.shape[0]
-    spans = [(0, 0, places), (-1, 0, places), (1, 0, places), (-2, 0, places), (2, 0, places)]
-    spans += [(-3, 0, places), (3, 0, places), (4, 0, places // 2), (4, places // 2, places // 2)]
+    sign = 1 - 2 * (place[1] % 2)
+    spans = [(0, 0, places)]
+    for k in (1, 2, 3):
+        spans += [(k, 0, places), (-k, 0, places)]
+    spans += [(4, 0, places // 2), (4, places // 2, places // 2)]
     pairs = []
     for piece, (k, low, count) in zip(pieces, spans):
-        z = (place[1] + k + NZ) % NZ
+        z = (place[1] + sign * k + NZ) % NZ
         at = pl.ds(pl.multiple_of(z * rows, rows), rows)
         pairs.append((piece, weight.at[pl.ds(low, count), at]))
     incoming = copies_of(pairs, sw)
@@ -277,7 +280,7 @@
 
 def pair_kernel(place, keep_ref, got_ref, *outs):
     for j in range(4):
-        at = (place[1] // 2 + j) % 4
+        at = (place[1] // 2) ^ j
         total = keep_ref[at] + got_ref[at].astype(F32)
         outs[j][...] = total.astype(outs[j].dtype)
 
@@ -342,16 +345,20 @@
     return lax.all_to_all(array, axes, 0, 0, tiled=True)
 
 
-def along_z(array, k):
-    return lax.ppermute(array, "z", [(z, (z + k) % NZ) for z in range(NZ)])
+def pair_z(array, distance):
+    return lax.ppermute(array, "z", [(z, z ^ distance) for z in range(NZ)])
+
+
+def pair_odd(array):
+    return lax.ppermute(array, "z", [(z, (((z + 1) ^ 1) - 1) % NZ) for z in range(NZ)])
 
 
 def gather_near(tiles, shape):
     return exchange(tiles, PLANE).reshape((NY * NX,) + shape)
 
 
-def ring_step(up, down, other):
-    return along_z(after(up, other), 1), along_z(after(down, other), -1)
+def ring_step(even, odd, other):
+    return pair_z(after(odd, other), 1), pair_odd(after(even, other))
 
 
 def along(array, k, far):
@@ -372,7 +379,7 @@
 
 
 def reduce_last(parts, attended):
-    moved = [along_z(parts[j], 2 * j) for j in (1, 2, 3)]
+    moved = [pair_z(parts[j], 2 * j) for j in (1, 2, 3)]
     total = parts[0] + after(moved[0], attended).astype(F32)
     return total + moved[1].astype(F32) + moved[2].astype(F32)
 
@@ -403,11 +410,11 @@
     second = ring_step(*first, away[0])
     far_sums = add_far(place, [here] + [along(away[k - 1], k, True) for k in (1, 2, 3)])
     keep, send = add_near(place, spread(far_sums, False))
-    got = lax.ppermute(send, "z", [(z, z ^ 1) for z in range(NZ)])
+    got = pair_z(send, 1)
     sums = add_pair(place, keep, got)
     third = ring_step(*second, near)
     half = near.shape[0] // 2
-    last = ring_step(third[0][:half], third[1][half:], far_sums[0])
+    last = ring_step(third[0][half:], third[1][:half], far_sums[0])
     pieces = [near, *first, *second, *third, last[0], after(last[1], sums[1])]
     values_own, values_other = partial_values(place, activations, act_got, pieces)
     attended = attend(probability, values_own, swap_cores(values_other), kv_heads)

time: 98.4 us -> 98.5 us (level)
  starting transfers between devices: 42.9 us -> 36.4 us
  waiting for transfers between devices: 24.1 us -> 30.5 us
    ppermute x12, starting transfers between devices: 22 us -> 14.9 us  [the longest x8 7.51 us: pair_z(): return lax.ppermute(array, 'z', [(z, z ^ distance) for z in range(NZ)])]
    ppermute x6, waiting for transfers between devices: 9.19 us -> 13.5 us  [along(): return lax.ppermute(array, AXES, pairs)]
    ppermute x12, waiting for transfers between devices: 13 us -> 15.2 us  [the longest x4 11.3 us: pair_odd(): lax.ppermute(array, 'z', [(z, ((z + 1 ^ 1) - 1) % NZ) for z in range(NZ)])]
  transfers between devices with their start and end apart: 22 -> 22, of which waited for: 6 -> 7; matrix products, arithmetic and copies ran while one was open for 1% -> 1% of each run, Pallas kernels for 19% -> 19%
where the time goes in v3:
time: 98.5 us; the launch traced here: 98.1 us
  starting transfers between devices  36.4 us (37%)
  waiting for transfers between devices  30.5 us (31%)
  Pallas kernels  24.7 us (25%)
  local copies, waits for them, and re-layouts  4.24 us (4%)
  other arithmetic  1.32 us (1%)
    ppermute x6, waiting for transfers between devices, along(): return lax.ppermute(array, AXES, pairs)  13.5 us
    ppermute x4, waiting for transfers between devices, pair_odd(): lax.ppermute(array, 'z', [(z, ((z + 1 ^ 1) - 1) % NZ) for z in range(NZ)])  11.3 us
    pallas_call x1, Pallas kernels, attention_weights(): pl.pallas_call(functools.partial(weights_kernel, head_dim), out_shape=(ja...  8.83 us
    ppermute x6, starting transfers between devices, along(): return lax.ppermute(array, AXES, pairs)  8.77 us
    ppermute x3, starting transfers between devices, swap_cores(): return lax.ppermute(array, 'c', [(0, 1), (1, 0)])  7.68 us
    ppermute x8, starting transfers between devices, pair_z(): return lax.ppermute(array, 'z', [(z, z ^ distance) for z in range(NZ)])  7.51 us
    ppermute x4, starting transfers between devices, pair_odd(): lax.ppermute(array, 'z', [(z, ((z + 1 ^ 1) - 1) % NZ) for z in range(NZ)])  7.39 us
    all_to_all x1, starting transfers between devices, exchange(): return lax.all_to_all(array, axes, 0, 0, tiled=True)  5.02 us
  transfers between devices with their start and end apart: 22, of which 7 were waited for; matrix products, arithmetic and copies ran while one was open for 1% of the time, Pallas kernels for 19%

profile of v3, /device:TPU:1, one launch (start us, length us, event | category | flops | bytes accessed | tf_op | source)
XLA Modules:
  0.0 98.1 jit_solution(18328548109464788157)
XLA Ops:
  1.3 3.2 %other_half.1 = bf16[256,4096]{1,0:T(8,128)(2,1)} custom-call(s32[4]{0:T(128)} %pad_add_fusion.place, bf16[256,8192]{1,0:T(8,128)(2,1)} %own_ref.5), custom_call_target="tpu_custom_call" | custom-call | bytes 4194304 | tf_op jit(solution)/shard_map/other_half/pallas_call | solution.py:63
  4.5 3.3 %collective-permute-start = (bf16[256,4096]{1,0:T(8,128)(2,1)}, bf16[256,4096]{1,0:T(8,128)(2,1)S(1)}, u32[]{:S(2)}, u32[]{:S(2)}) collective-permute-start(bf16[256,4096]{1,0:T(8,128)(2,1)} %other_half.1), channel_id=1, source_target_pairs={{0,16},{16,0},{1,17},{17,1},{2,18},{18,2},{3,19},{19,3},{4,20},{20... | collective-permute-start | bytes 6291464 | tf_op jit(solution)/shard_map/ppermute | solution.py:18
  8.0 0.9 tile.2
  8.9 5.0 %all-to-all-start = ((bf16[16,32,512]{2,1,0:T(8,128)(2,1)}), bf16[16,32,512]{2,1,0:T(8,128)(2,1)S(1)}, u32[]{:S(2)}, u32[]{:S(2)}) async-start(bf16[16,32,512]{2,1,0:T(8,128)(2,1)} %tile.2), calls=%async_computation | async-start | bytes 1048576 | tf_op jit(solution)/shard_map/all_to_all | solution.py:345
  14.0 8.8 %attention_weights.1 = (bf16[32,256,256]{2,1,0:T(8,128)(2,1)}, bf16[256,512]{1,0:T(8,128)(2,1)}) custom-call(bf16[256,4096]{1,0:T(8,128)(2,1)} %q_hbm.1, bf16[256,512]{1,0:T(8,128)(2,1)} %k_ref.1, bf16[256,4096]{1,0:T(8,128)(2,1)} %cot_hbm.1, s32[1,256]{1,0:T(1,128)} %segment_ref.1), custom_call_target="tpu_custom_call" | custom-call | flops 1073741824 | bytes 16777216 | tf_op jit(solution)/shard_map/attention_weights/pallas_call | solution.py:128
  23.2 1.5 %collective-permute-done.1.dvg_ref = bf16[256,512]{1,0:T(8,128)(2,1)S(1)} collective-permute-done((bf16[256,512]{1,0:T(8,128)(2,1)}, bf16[256,512]{1,0:T(8,128)(2,1)S(1)}, u32[]{:S(2)}, u32[]{:S(2)}) %collective-permute-start.1) | collective-permute-done | bytes 262176 | tf_op jit(solution)/shard_map/ppermute | solution.py:18
  25.0 1.6 %collective-permute-start.2 = (bf16[16,32,512]{2,1,0:T(8,128)(2,1)S(1)}, bf16[16,32,512]{2,1,0:T(8,128)(2,1)S(1)}, u32[]{:S(2)}, u32[]{:S(2)}) collective-permute-start(bf16[16,32,512]{2,1,0:T(8,128)(2,1)S(1)} %all-to-all-done.refs_0_), channel_id=1, source_target_pairs={{0,1},{1,0},{2,3},{3,2},{4,5},{5,4},{6,7},{7,6},{8,9},{9,8},{10,11... | collective-permute-start | bytes 1572872 | tf_op jit(solution)/shard_map/ppermute | solution.py:349
  26.7 4.7 %collective-permute-start.3 = (bf16[16,32,512]{2,1,0:T(8,128)(2,1)S(1)}, bf16[16,32,512]{2,1,0:T(8,128)(2,1)S(1)}, u32[]{:S(2)}, u32[]{:S(2)}) collective-permute-start(bf16[16,32,512]{2,1,0:T(8,128)(2,1)S(1)} %all-to-all-done.refs_0_), channel_id=1, source_target_pairs={{0,7},{1,2},{2,1},{3,4},{4,3},{5,6},{6,5},{7,0},{8,15},{9,10},{10,... | collective-permute-start | bytes 1572872 | tf_op jit(solution)/shard_map/ppermute | solution.py:353
  31.3 2.2 %copy-done = bf16[256,8192]{1,0:T(8,128)(2,1)S(1)} copy-done((bf16[256,8192]{1,0:T(8,128)(2,1)S(1)}, bf16[256,8192]{1,0:T(8,128)(2,1)}, u32[]{:S(2)}) %copy-start) | copy-done | bytes 4194328
  33.5 0.9 copy-done.3
  34.5 2.4 %product.2 = (bf16[4,512,256]{2,1,0:T(8,128)(2,1)S(1)}, bf16[4,512,256]{2,1,0:T(8,128)(2,1)S(1)}, bf16[4,512,256]{2,1,0:T(8,128)(2,1)S(1)}) custom-call(s32[4]{0:T(128)S(1)} %copy-done.4, bf16[256,8192]{1,0:T(8,128)(2,1)S(1)} %copy-done, bf16[256,4096]{1,0:T(8,128)(2,1)S(1)} %collective-permute-done.got_ref, bf16[256,512]{1,0:T(8,128)(2,1)S(1)} %copy-done.3, ...), custom_call_target="tpu_custom_call" | custom-call | flops 1610612736 | bytes 9437184 | tf_op jit(solution)/shard_map/product/pallas_call | solution.py:167
  36.9 1.3 %collective-permute-start.8 = (bf16[4,512,256]{2,1,0:T(8,128)(2,1)S(1)}, bf16[4,512,256]{2,1,0:T(8,128)(2,1)S(1)}, u32[]{:S(2)}, u32[]{:S(2)}) collective-permute-start(bf16[4,512,256]{2,1,0:T(8,128)(2,1)S(1)} %get-tuple-element.33), channel_id=1, source_target_pairs={{0,64},{1,65},{2,66},{3,67},{4,68},{5,69},{6,70},{7,71},{16,24},{1... | collective-permute-start | bytes 3145736 | tf_op jit(solution)/shard_map/ppermute | solution.py:374
  38.1 1.5 %collective-permute-start.10 = (bf16[4,512,256]{2,1,0:T(8,128)(2,1)S(1)}, bf16[4,512,256]{2,1,0:T(8,128)(2,1)S(1)}, u32[]{:S(2)}, u32[]{:S(2)}) collective-permute-start(bf16[4,512,256]{2,1,0:T(8,128)(2,1)S(1)} %get-tuple-element.39), channel_id=1, source_target_pairs={{0,192},{1,193},{2,194},{3,195},{4,196},{5,197},{6,198},{7,199},{1... | collective-permute-start | bytes 3145736 | tf_op jit(solution)/shard_map/ppermute | solution.py:374
  39.6 1.5 %collective-permute-start.9 = (bf16[4,512,256]{2,1,0:T(8,128)(2,1)S(1)}, bf16[4,512,256]{2,1,0:T(8,128)(2,1)S(1)}, u32[]{:S(2)}, u32[]{:S(2)}) collective-permute-start(bf16[4,512,256]{2,1,0:T(8,128)(2,1)S(1)} %get-tuple-element.38), channel_id=1, source_target_pairs={{0,128},{1,129},{2,130},{3,131},{4,132},{5,133},{6,134},{7,135},{1... | collective-permute-start | bytes 3145736 | tf_op jit(solution)/shard_map/ppermute | solution.py:374
  41.1 1.5 %collective-permute-start.5 = (bf16[16,32,512]{2,1,0:T(8,128)(2,1)S(1)}, bf16[16,32,512]{2,1,0:T(8,128)(2,1)S(1)}, u32[]{:S(2)}, u32[]{:S(2)}) collective-permute-start(bf16[16,32,512]{2,1,0:T(8,128)(2,1)S(1)} %collective-permute-done.2.refs_1_), channel_id=1, source_target_pairs={{0,7},{1,2},{2,1},{3,4},{4,3},{5,6},{6,5},{7,0},{8,15},{9,10},{10,... | collective-permute-start | bytes 1572872 | tf_op jit(solution)/shard_map/ppermute | solution.py:353
  42.6 11.3 %collective-permute-done.5.refs_4_ = bf16[16,32,512]{2,1,0:T(8,128)(2,1)S(1)} collective-permute-done((bf16[16,32,512]{2,1,0:T(8,128)(2,1)S(1)}, bf16[16,32,512]{2,1,0:T(8,128)(2,1)S(1)}, u32[]{:S(2)}, u32[]{:S(2)}) %collective-permute-start.5) | collective-permute-done | bytes 524320 | tf_op jit(solution)/shard_map/ppermute | solution.py:353
  53.9 1.1 %collective-permute-start.7 = (bf16[16,32,512]{2,1,0:T(8,128)(2,1)S(1)}, bf16[16,32,512]{2,1,0:T(8,128)(2,1)S(1)}, u32[]{:S(2)}, u32[]{:S(2)}) collective-permute-start(bf16[16,32,512]{2,1,0:T(8,128)(2,1)S(1)} %collective-permute-done.4.refs_3_), channel_id=1, source_target_pairs={{0,7},{1,2},{2,1},{3,4},{4,3},{5,6},{6,5},{7,0},{8,15},{9,10},{10,... | collective-permute-start | bytes 1572872 | tf_op jit(solution)/shard_map/ppermute | solution.py:353
  55.1 1.3 %product.3.refs_0_ = bf16[4,512,256]{2,1,0:T(8,128)(2,1)S(1)} custom-call(s32[4]{0:T(128)S(1)} %copy-done.4, bf16[256,8192]{1,0:T(8,128)(2,1)S(1)} %copy-done, bf16[256,4096]{1,0:T(8,128)(2,1)S(1)} %collective-permute-done.got_ref, bf16[256,512]{1,0:T(8,128)(2,1)S(1)} %copy-done.3, bf16[256,512]{1,0:T(8,128)(2,1)S(1)} %collective-permute-done.1.dvg_ref), custom_call_target="tpu_custom_call" | custom-call | flops 536870912 | bytes 3145728 | tf_op jit(solution)/shard_map/product/pallas_call | solution.py:167
  56.4 7.8 %collective-permute-done.9.refs_2_ = bf16[4,512,256]{2,1,0:T(8,128)(2,1)S(1)} collective-permute-done((bf16[4,512,256]{2,1,0:T(8,128)(2,1)S(1)}, bf16[4,512,256]{2,1,0:T(8,128)(2,1)S(1)}, u32[]{:S(2)}, u32[]{:S(2)}) %collective-permute-start.9) | collective-permute-done | bytes 1048608 | tf_op jit(solution)/shard_map/ppermute | solution.py:374
  64.2 1.1 %add_far.1 = (bf16[512,256]{1,0:T(8,128)(2,1)S(1)}, bf16[512,256]{1,0:T(8,128)(2,1)S(1)}, bf16[512,256]{1,0:T(8,128)(2,1)S(1)}, bf16[512,256]{1,0:T(8,128)(2,1)S(1)}) custom-call(s32[4]{0:T(128)S(1)} %copy-done.4, bf16[4,512,256]{2,1,0:T(8,128)(2,1)S(1)} %product.3.refs_0_, bf16[4,512,256]{2,1,0:T(8,128)(2,1)S(1)} %collective-permute-done.8.refs_1_, ...), custom_call_target="tpu_custom_call" | custom-call | flops 2097152 | bytes 5242880 | tf_op jit(solution)/shard_map/add_far/pallas_call | solution.py:239
  65.3 1.0 %collective-permute-start.13 = (bf16[512,256]{1,0:T(8,128)(2,1)S(1)}, bf16[512,256]{1,0:T(8,128)(2,1)S(1)}, u32[]{:S(2)}, u32[]{:S(2)}) collective-permute-start(bf16[512,256]{1,0:T(8,128)(2,1)S(1)} %get-tuple-element.43), channel_id=1, source_target_pairs={{0,8},{1,9},{2,10},{3,11},{4,12},{5,13},{6,14},{7,15},{16,80},{17,... | collective-permute-start | bytes 786440 | tf_op jit(solution)/shard_map/ppermute | solution.py:374
  66.3 2.7 %collective-permute-start.14 = (bf16[512,256]{1,0:T(8,128)(2,1)S(1)}, bf16[512,256]{1,0:T(8,128)(2,1)S(1)}, u32[]{:S(2)}, u32[]{:S(2)}) collective-permute-start(bf16[512,256]{1,0:T(8,128)(2,1)S(1)} %get-tuple-element.44), channel_id=1, source_target_pairs={{0,32},{1,33},{2,34},{3,35},{4,36},{5,37},{6,38},{7,39},{16,144},{... | collective-permute-start | bytes 786440 | tf_op jit(solution)/shard_map/ppermute | solution.py:374
  69.0 0.9 collective-permute-start.15
  70.1 2.0 %collective-permute-done.13.refs_1_ = bf16[512,256]{1,0:T(8,128)(2,1)S(1)} collective-permute-done((bf16[512,256]{1,0:T(8,128)(2,1)S(1)}, bf16[512,256]{1,0:T(8,128)(2,1)S(1)}, u32[]{:S(2)}, u32[]{:S(2)}) %collective-permute-start.13) | collective-permute-done | bytes 262176 | tf_op jit(solution)/shard_map/ppermute | solution.py:374
  72.1 3.7 %collective-permute-done.14.refs_2_ = bf16[512,256]{1,0:T(8,128)(2,1)S(1)} collective-permute-done((bf16[512,256]{1,0:T(8,128)(2,1)S(1)}, bf16[512,256]{1,0:T(8,128)(2,1)S(1)}, u32[]{:S(2)}, u32[]{:S(2)}) %collective-permute-start.14) | collective-permute-done | bytes 262176 | tf_op jit(solution)/shard_map/ppermute | solution.py:374
  75.8 0.8 add_near.1
  76.8 3.8 %collective-permute-done.16.got_ref = bf16[4,32,512]{2,1,0:T(8,128)(2,1)S(1)} collective-permute-done((bf16[4,32,512]{2,1,0:T(8,128)(2,1)S(1)}, bf16[4,32,512]{2,1,0:T(8,128)(2,1)S(1)}, u32[]{:S(2)}, u32[]{:S(2)}) %collective-permute-start.16) | collective-permute-done | bytes 131104 | tf_op jit(solution)/shard_map/ppermute | solution.py:349
  81.2 3.3 %partial_values.1 = (f32[256,512]{1,0:T(8,128)S(1)}, f32[256,512]{1,0:T(8,128)S(1)}) custom-call(s32[4]{0:T(128)S(1)} %copy-done.4, bf16[256,8192]{1,0:T(8,128)(2,1)S(1)} %copy-done.1, bf16[256,4096]{1,0:T(8,128)(2,1)S(1)} %collective-permute-done.got_ref, bf16[16,32,512]{2,1,0:T(8,128)(2,1)S(1)} %all-to-all-done.refs_0_, ...), custom_call_target="tpu_custom_call" | custom-call | flops 2147483648 | bytes 12582912 | tf_op jit(solution)/shard_map/partial_values/pallas_call | solution.py:211
  84.5 4.0 %collective-permute-start.17 = (f32[256,512]{1,0:T(8,128)S(1)}, f32[256,512]{1,0:T(8,128)S(1)}, u32[]{:S(2)}, u32[]{:S(2)}) collective-permute-start(f32[256,512]{1,0:T(8,128)S(1)} %get-tuple-element.51), channel_id=1, source_target_pairs={{0,16},{16,0},{1,17},{17,1},{2,18},{18,2},{3,19},{19,3},{4,20},{20... | collective-permute-start | bytes 1572872 | tf_op jit(solution)/shard_map/ppermute | solution.py:18
  88.7 3.1 %collective-permute-start.19 = (bf16[32,512]{1,0:T(8,128)(2,1)S(1)}, bf16[32,512]{1,0:T(8,128)(2,1)S(1)}, u32[]{:S(2)}, u32[]{:S(2)}) collective-permute-start(bf16[32,512]{1,0:T(8,128)(2,1)S(1)} %get-tuple-element.54), channel_id=1, source_target_pairs={{0,4},{1,5},{2,6},{3,7},{4,0},{5,1},{6,2},{7,3},{8,12},{9,13},{10,... | collective-permute-start | bytes 98312 | tf_op jit(solution)/shard_map/ppermute | solution.py:349
  91.7 2.4 %collective-permute-start.20 = (bf16[32,512]{1,0:T(8,128)(2,1)S(1)}, bf16[32,512]{1,0:T(8,128)(2,1)S(1)}, u32[]{:S(2)}, u32[]{:S(2)}) collective-permute-start(bf16[32,512]{1,0:T(8,128)(2,1)S(1)} %get-tuple-element.55), channel_id=1, source_target_pairs={{0,6},{1,7},{2,4},{3,5},{4,2},{5,3},{6,0},{7,1},{8,14},{9,15},{10,... | collective-permute-start | bytes 98312 | tf_op jit(solution)/shard_map/ppermute | solution.py:349
  94.2 3.2 %attend.1 = bf16[256,4096]{1,0:T(8,128)(2,1)} custom-call(bf16[32,256,256]{2,1,0:T(8,128)(2,1)S(1)} %copy-done.2, f32[256,512]{1,0:T(8,128)S(1)} %get-tuple-element.50.vo_ref, f32[256,512]{1,0:T(8,128)S(1)} %collective-permute-done.17.vg_ref), custom_call_target="tpu_custom_call" | custom-call | flops 536870912 | bytes 8388608 | tf_op jit(solution)/shard_map/attend/pallas_call | solution.py:324
  (43 shorter events, 3.4 us)
Async XLA Ops:
  1.3 6.5 %copy-start.6 = (f32[32,4]{0,1:T(4,128)S(1)}, f32[32,4]{0,1:T(4,128)}, u32[]{:S(2)}) copy-start(f32[32,4]{0,1:T(4,128)} %param.13) | copy-start | bytes 1540
  1.3 6.7 %copy-start.5 = (bf16[32,512]{1,0:T(8,128)(2,1)S(1)}, bf16[32,512]{1,0:T(8,128)(2,1)}, u32[]{:S(2)}) copy-start(bf16[32,512]{1,0:T(8,128)(2,1)} %param.12) | copy-start | bytes 98308
  4.5 26.8 %collective-permute-start = (bf16[256,4096]{1,0:T(8,128)(2,1)}, bf16[256,4096]{1,0:T(8,128)(2,1)S(1)}, u32[]{:S(2)}, u32[]{:S(2)}) collective-permute-start(bf16[256,4096]{1,0:T(8,128)(2,1)} %other_half.1), channel_id=1, source_target_pairs={{0,16},{16,0},{1,17},{17,1},{2,18},{18,2},{3,19},{19,3},{4,20},{20... | collective-permute-start | bytes 6291464 | tf_op jit(solution)/shard_map/ppermute | solution.py:18
  8.9 16.1 %all-to-all-start = ((bf16[16,32,512]{2,1,0:T(8,128)(2,1)}), bf16[16,32,512]{2,1,0:T(8,128)(2,1)S(1)}, u32[]{:S(2)}, u32[]{:S(2)}) async-start(bf16[16,32,512]{2,1,0:T(8,128)(2,1)} %tile.2), calls=%async_computation | async-start | bytes 1048576 | tf_op jit(solution)/shard_map/all_to_all | solution.py:345
  13.9 17.4 %copy-start.4 = (s32[4]{0:T(128)S(1)}, s32[4]{0:T(128)}, u32[]{:S(2)}) copy-start(s32[4]{0:T(128)} %pad_add_fusion.place) | copy-start | bytes 52
  22.8 1.8 %collective-permute-start.1 = (bf16[256,512]{1,0:T(8,128)(2,1)}, bf16[256,512]{1,0:T(8,128)(2,1)S(1)}, u32[]{:S(2)}, u32[]{:S(2)}) collective-permute-start(bf16[256,512]{1,0:T(8,128)(2,1)} %get-tuple-element.30.dvo_ref), channel_id=1, source_target_pairs={{0,16},{16,0},{1,17},{17,1},{2,18},{18,2},{3,19},{19,3},{4,20},{20... | collective-permute-start | bytes 786440 | tf_op jit(solution)/shard_map/ppermute | solution.py:18
  25.0 16.1 %collective-permute-start.2 = (bf16[16,32,512]{2,1,0:T(8,128)(2,1)S(1)}, bf16[16,32,512]{2,1,0:T(8,128)(2,1)S(1)}, u32[]{:S(2)}, u32[]{:S(2)}) collective-permute-start(bf16[16,32,512]{2,1,0:T(8,128)(2,1)S(1)} %all-to-all-done.refs_0_), channel_id=1, source_target_pairs={{0,1},{1,0},{2,3},{3,2},{4,5},{5,4},{6,7},{7,6},{8,9},{9,8},{10,11... | collective-permute-start | bytes 1572872 | tf_op jit(solution)/shard_map/ppermute | solution.py:349
  26.7 15.9 %collective-permute-start.3 = (bf16[16,32,512]{2,1,0:T(8,128)(2,1)S(1)}, bf16[16,32,512]{2,1,0:T(8,128)(2,1)S(1)}, u32[]{:S(2)}, u32[]{:S(2)}) collective-permute-start(bf16[16,32,512]{2,1,0:T(8,128)(2,1)S(1)} %all-to-all-done.refs_0_), channel_id=1, source_target_pairs={{0,7},{1,2},{2,1},{3,4},{4,3},{5,6},{6,5},{7,0},{8,15},{9,10},{10,... | collective-permute-start | bytes 1572872 | tf_op jit(solution)/shard_map/ppermute | solution.py:353
  31.3 2.2 %copy-start = (bf16[256,8192]{1,0:T(8,128)(2,1)S(1)}, bf16[256,8192]{1,0:T(8,128)(2,1)}, u32[]{:S(2)}) copy-start(bf16[256,8192]{1,0:T(8,128)(2,1)} %own_ref.5) | copy-start | bytes 12582916
  33.5 0.9 copy-start.3
  36.9 19.5 %collective-permute-start.8 = (bf16[4,512,256]{2,1,0:T(8,128)(2,1)S(1)}, bf16[4,512,256]{2,1,0:T(8,128)(2,1)S(1)}, u32[]{:S(2)}, u32[]{:S(2)}) collective-permute-start(bf16[4,512,256]{2,1,0:T(8,128)(2,1)S(1)} %get-tuple-element.33), channel_id=1, source_target_pairs={{0,64},{1,65},{2,66},{3,67},{4,68},{5,69},{6,70},{7,71},{16,24},{1... | collective-permute-start | bytes 3145736 | tf_op jit(solution)/shard_map/ppermute | solution.py:374
  38.1 18.3 %collective-permute-start.10 = (bf16[4,512,256]{2,1,0:T(8,128)(2,1)S(1)}, bf16[4,512,256]{2,1,0:T(8,128)(2,1)S(1)}, u32[]{:S(2)}, u32[]{:S(2)}) collective-permute-start(bf16[4,512,256]{2,1,0:T(8,128)(2,1)S(1)} %get-tuple-element.39), channel_id=1, source_target_pairs={{0,192},{1,193},{2,194},{3,195},{4,196},{5,197},{6,198},{7,199},{1... | collective-permute-start | bytes 3145736 | tf_op jit(solution)/shard_map/ppermute | solution.py:374
  39.6 24.6 %collective-permute-start.9 = (bf16[4,512,256]{2,1,0:T(8,128)(2,1)S(1)}, bf16[4,512,256]{2,1,0:T(8,128)(2,1)S(1)}, u32[]{:S(2)}, u32[]{:S(2)}) collective-permute-start(bf16[4,512,256]{2,1,0:T(8,128)(2,1)S(1)} %get-tuple-element.38), channel_id=1, source_target_pairs={{0,128},{1,129},{2,130},{3,131},{4,132},{5,133},{6,134},{7,135},{1... | collective-permute-start | bytes 3145736 | tf_op jit(solution)/shard_map/ppermute | solution.py:374
  41.1 12.8 %collective-permute-start.5 = (bf16[16,32,512]{2,1,0:T(8,128)(2,1)S(1)}, bf16[16,32,512]{2,1,0:T(8,128)(2,1)S(1)}, u32[]{:S(2)}, u32[]{:S(2)}) collective-permute-start(bf16[16,32,512]{2,1,0:T(8,128)(2,1)S(1)} %collective-permute-done.2.refs_1_), channel_id=1, source_target_pairs={{0,7},{1,2},{2,1},{3,4},{4,3},{5,6},{6,5},{7,0},{8,15},{9,10},{10,... | collective-permute-start | bytes 1572872 | tf_op jit(solution)/shard_map/ppermute | solution.py:353
  42.6 11.3 %collective-permute-start.4 = (bf16[16,32,512]{2,1,0:T(8,128)(2,1)S(1)}, bf16[16,32,512]{2,1,0:T(8,128)(2,1)S(1)}, u32[]{:S(2)}, u32[]{:S(2)}) collective-permute-start(bf16[16,32,512]{2,1,0:T(8,128)(2,1)S(1)} %collective-permute-done.3.refs_2_), channel_id=1, source_target_pairs={{0,1},{1,0},{2,3},{3,2},{4,5},{5,4},{6,7},{7,6},{8,9},{9,8},{10,11... | collective-permute-start | bytes 1572872 | tf_op jit(solution)/shard_map/ppermute | solution.py:349
  53.9 15.9 %collective-permute-start.6 = (bf16[16,32,512]{2,1,0:T(8,128)(2,1)S(1)}, bf16[16,32,512]{2,1,0:T(8,128)(2,1)S(1)}, u32[]{:S(2)}, u32[]{:S(2)}) collective-permute-start(bf16[16,32,512]{2,1,0:T(8,128)(2,1)S(1)} %collective-permute-done.5.refs_4_), channel_id=1, source_target_pairs={{0,1},{1,0},{2,3},{3,2},{4,5},{5,4},{6,7},{7,6},{8,9},{9,8},{10,11... | collective-permute-start | bytes 1572872 | tf_op jit(solution)/shard_map/ppermute | solution.py:349
  53.9 16.1 %collective-permute-start.7 = (bf16[16,32,512]{2,1,0:T(8,128)(2,1)S(1)}, bf16[16,32,512]{2,1,0:T(8,128)(2,1)S(1)}, u32[]{:S(2)}, u32[]{:S(2)}) collective-permute-start(bf16[16,32,512]{2,1,0:T(8,128)(2,1)S(1)} %collective-permute-done.4.refs_3_), channel_id=1, source_target_pairs={{0,7},{1,2},{2,1},{3,4},{4,3},{5,6},{6,5},{7,0},{8,15},{9,10},{10,... | collective-permute-start | bytes 1572872 | tf_op jit(solution)/shard_map/ppermute | solution.py:353
  64.2 16.9 %copy-start.1 = (bf16[256,8192]{1,0:T(8,128)(2,1)S(1)}, bf16[256,8192]{1,0:T(8,128)(2,1)}, u32[]{:S(2)}) copy-start(bf16[256,8192]{1,0:T(8,128)(2,1)} %own_ref.5) | copy-start | bytes 12582916
  65.3 6.8 %collective-permute-start.13 = (bf16[512,256]{1,0:T(8,128)(2,1)S(1)}, bf16[512,256]{1,0:T(8,128)(2,1)S(1)}, u32[]{:S(2)}, u32[]{:S(2)}) collective-permute-start(bf16[512,256]{1,0:T(8,128)(2,1)S(1)} %get-tuple-element.43), channel_id=1, source_target_pairs={{0,8},{1,9},{2,10},{3,11},{4,12},{5,13},{6,14},{7,15},{16,80},{17,... | collective-permute-start | bytes 786440 | tf_op jit(solution)/shard_map/ppermute | solution.py:374
  66.3 9.5 %collective-permute-start.14 = (bf16[512,256]{1,0:T(8,128)(2,1)S(1)}, bf16[512,256]{1,0:T(8,128)(2,1)S(1)}, u32[]{:S(2)}, u32[]{:S(2)}) collective-permute-start(bf16[512,256]{1,0:T(8,128)(2,1)S(1)} %get-tuple-element.44), channel_id=1, source_target_pairs={{0,32},{1,33},{2,34},{3,35},{4,36},{5,37},{6,38},{7,39},{16,144},{... | collective-permute-start | bytes 786440 | tf_op jit(solution)/shard_map/ppermute | solution.py:374
  69.0 6.9 %collective-permute-start.15 = (bf16[512,256]{1,0:T(8,128)(2,1)S(1)}, bf16[512,256]{1,0:T(8,128)(2,1)S(1)}, u32[]{:S(2)}, u32[]{:S(2)}) collective-permute-start(bf16[512,256]{1,0:T(8,128)(2,1)S(1)} %get-tuple-element.45), channel_id=1, source_target_pairs={{0,40},{1,41},{2,42},{3,43},{4,44},{5,45},{6,46},{7,47},{16,208},{... | collective-permute-start | bytes 786440 | tf_op jit(solution)/shard_map/ppermute | solution.py:374
  69.9 11.3 %collective-permute-start.12 = (bf16[8,32,512]{2,1,0:T(8,128)(2,1)S(1)}, bf16[8,32,512]{2,1,0:T(8,128)(2,1)S(1)}, u32[]{:S(2)}, u32[]{:S(2)}) collective-permute-start(bf16[8,32,512]{2,1,0:T(8,128)(2,1)S(1)} %slice.9), channel_id=1, source_target_pairs={{0,7},{1,2},{2,1},{3,4},{4,3},{5,6},{6,5},{7,0},{8,15},{9,10},{10,... | collective-permute-start | bytes 786440 | tf_op jit(solution)/shard_map/ppermute | solution.py:353
  70.0 11.1 %collective-permute-start.11 = (bf16[8,32,512]{2,1,0:T(8,128)(2,1)S(1)}, bf16[8,32,512]{2,1,0:T(8,128)(2,1)S(1)}, u32[]{:S(2)}, u32[]{:S(2)}) collective-permute-start(bf16[8,32,512]{2,1,0:T(8,128)(2,1)S(1)} %slice.8), channel_id=1, source_target_pairs={{0,1},{1,0},{2,3},{3,2},{4,5},{5,4},{6,7},{7,6},{8,9},{9,8},{10,11... | collective-permute-start | bytes 786440 | tf_op jit(solution)/shard_map/ppermute | solution.py:349
  76.7 3.9 %collective-permute-start.16 = (bf16[4,32,512]{2,1,0:T(8,128)(2,1)S(1)}, bf16[4,32,512]{2,1,0:T(8,128)(2,1)S(1)}, u32[]{:S(2)}, u32[]{:S(2)}) collective-permute-start(bf16[4,32,512]{2,1,0:T(8,128)(2,1)S(1)} %get-tuple-element.47), channel_id=1, source_target_pairs={{0,1},{1,0},{2,3},{3,2},{4,5},{5,4},{6,7},{7,6},{8,9},{9,8},{10,11... | collective-permute-start | bytes 393224 | tf_op jit(solution)/shard_map/ppermute | solution.py:349
  81.2 13.0 %copy-start.2 = (bf16[32,256,256]{2,1,0:T(8,128)(2,1)S(1)}, bf16[32,256,256]{2,1,0:T(8,128)(2,1)}, u32[]{:S(2)}) copy-start(bf16[32,256,256]{2,1,0:T(8,128)(2,1)} %get-tuple-element.29.p_hbm) | copy-start | bytes 12582916
  84.5 9.7 %collective-permute-start.17 = (f32[256,512]{1,0:T(8,128)S(1)}, f32[256,512]{1,0:T(8,128)S(1)}, u32[]{:S(2)}, u32[]{:S(2)}) collective-permute-start(f32[256,512]{1,0:T(8,128)S(1)} %get-tuple-element.51), channel_id=1, source_target_pairs={{0,16},{16,0},{1,17},{17,1},{2,18},{18,2},{3,19},{19,3},{4,20},{20... | collective-permute-start | bytes 1572872 | tf_op jit(solution)/shard_map/ppermute | solution.py:18
  88.5 8.9 %collective-permute-start.18 = (bf16[32,512]{1,0:T(8,128)(2,1)S(1)}, bf16[32,512]{1,0:T(8,128)(2,1)S(1)}, u32[]{:S(2)}, u32[]{:S(2)}) collective-permute-start(bf16[32,512]{1,0:T(8,128)(2,1)S(1)} %get-tuple-element.48), channel_id=1, source_target_pairs={{0,2},{1,3},{2,0},{3,1},{4,6},{5,7},{6,4},{7,5},{8,10},{9,11},{10,... | collective-permute-start | bytes 98312 | tf_op jit(solution)/shard_map/ppermute | solution.py:349
  88.7 8.8 %collective-permute-start.19 = (bf16[32,512]{1,0:T(8,128)(2,1)S(1)}, bf16[32,512]{1,0:T(8,128)(2,1)S(1)}, u32[]{:S(2)}, u32[]{:S(2)}) collective-permute-start(bf16[32,512]{1,0:T(8,128)(2,1)S(1)} %get-tuple-element.54), channel_id=1, source_target_pairs={{0,4},{1,5},{2,6},{3,7},{4,0},{5,1},{6,2},{7,3},{8,12},{9,13},{10,... | collective-permute-start | bytes 98312 | tf_op jit(solution)/shard_map/ppermute | solution.py:349
  91.7 5.7 %collective-permute-start.20 = (bf16[32,512]{1,0:T(8,128)(2,1)S(1)}, bf16[32,512]{1,0:T(8,128)(2,1)S(1)}, u32[]{:S(2)}, u32[]{:S(2)}) collective-permute-start(bf16[32,512]{1,0:T(8,128)(2,1)S(1)} %get-tuple-element.55), channel_id=1, source_target_pairs={{0,6},{1,7},{2,4},{3,5},{4,2},{5,3},{6,0},{7,1},{8,14},{9,15},{10,... | collective-permute-start | bytes 98312 | tf_op jit(solution)/shard_map/ppermute | solution.py:349
